TPU v7x, 512 devices: a whole 4x4x16 slice. The times are simulated.
512 devices in a mesh: dp: 64 (over z, y), table: 8 (over x, core).
Axes of the slice: x: 4, y: 4, z: 16, core: 2. Of those that a mesh axis runs over, the one named last changes fastest.
Arguments:
- token_slot: int32 [2, 512, 256], P(None, ('dp', 'table')), may hold values from 0 to 127, as said below
- seg_ids: int32 [2, 512, 256], P(None, ('dp', 'table')), may hold values from 0 to 3, never falling along the last dimension, each value on 1 to 128 neighbouring positions
- req_rows: int32 [2, 4096, 16], P(None, ('dp', 'table')), may hold values from 0 to 127, as said below
- cotangent: bfloat16 [2, 131072, 512], P(None, ('dp', 'table')), may hold values from -6 to 6
- uvqk_weight: bfloat16 [1024, 2048], P('dp'), may hold values from -0.1875 to 0.1875
- table: bfloat16 [1024, 1024], P('table'), may hold values from -6 to 6
- first_moment: float32 [1024, 1024], P('table'), may hold values from -6 to 6
- second_moment: float32 [1024, 1024], P('table'), may hold values from 0.1 to 1
- dup_count: int32 [64], replicated, may hold values from 0 to 8, as said below
- dup_target: int32 [64, 8], replicated, may hold values from 0 to 63
Outputs:
- new_rows: bfloat16 [1024, 1024], P('table')
- new_first: float32 [1024, 1024], P('table')
- new_second: float32 [1024, 1024], P('table')
Inputs may be any that keep to these rules, and one draw needn't show every extreme that they name: `token_slot`: every one of a device's 8 * 16 slots holds some token in each micro-step. `req_rows`: the 16 requests of one device to one shard in one micro-step are distinct rows. `dup_count`: each shard has exactly 8 live replicas for some owner shard, which may be itself.
All inputs are finite; a program needn't handle non-finite values.
Results may differ from a plain program's by a relative error of at most 0.014.
Values may be sent and summed in bfloat16 or wider, within the bound.
A program may use at most 64 MiB of HBM per device.

v0:
```python
import jax
import jax.numpy as jnp
from jax import lax
from jax.sharding import PartitionSpec as P

HEADS = 4
MICRO = 2


beta_one = 0.9
beta_two = 0.999
learn_rate = 0.1
adam_eps = 1e-08
norm_eps = 1e-05


def layer_norm(values):
    center = jnp.mean(values, axis=-1, keepdims=True)
    shifted = values - center
    spread = jnp.mean(shifted * shifted, axis=-1, keepdims=True)
    return shifted * lax.rsqrt(spread + norm_eps)


def hstu_block(inputs, weight, segment, heads):
    normed = layer_norm(inputs).astype(jnp.bfloat16)
    projected = jax.nn.silu(jnp.dot(normed, weight, preferred_element_type=jnp.float32))
    width = weight.shape[1] // 4
    count = inputs.shape[0]
    head_dim = width // heads
    gate = projected[:, :width]
    values = projected[:, width : 2 * width].astype(jnp.bfloat16).reshape(count, heads, head_dim)
    queries = (
        projected[:, 2 * width : 3 * width].astype(jnp.bfloat16).reshape(count, heads, head_dim)
    )
    keys_part = projected[:, 3 * width :].astype(jnp.bfloat16).reshape(count, heads, head_dim)
    scores = jnp.einsum(
        "thd,shd->hts", queries, keys_part, preferred_element_type=jnp.float32
    ) * head_dim ** (-0.5)
    same = segment[:, None] == segment[None, :]
    place = jnp.arange(count, dtype=jnp.int32)
    causal = place[:, None] >= place[None, :]
    masked = jnp.where(same & causal, 1.0, 0.0).astype(jnp.float32)
    history = jnp.sum(jnp.where(same, 1.0, 0.0).astype(jnp.float32), axis=1)
    attn = (jax.nn.silu(scores) * masked[None] / history[None, :, None]).astype(jnp.bfloat16)
    mixed = jnp.einsum("hts,shd->thd", attn, values, preferred_element_type=jnp.float32).reshape(
        count, width
    )
    return layer_norm(mixed) * gate


def consolidate(grad, first_moment, second_moment, dup_count, dup_target, shard_self, shards):
    first_step = beta_one * first_moment + (1.0 - beta_one) * grad
    second_step = beta_two * second_moment + (1.0 - beta_two) * grad * grad
    hot_rows, columns = grad.shape
    slots_each = dup_target.shape[1]
    owned = hot_rows - shards * slots_each
    counts = dup_count.reshape(shards, shards)
    targets = dup_target.reshape(shards, shards, slots_each)
    place = jnp.arange(slots_each, dtype=jnp.int32)
    incoming = lax.dynamic_index_in_dim(counts, shard_self, 1, keepdims=False)
    in_targets = lax.dynamic_index_in_dim(targets, shard_self, 1, keepdims=False).reshape(-1)
    in_live = jnp.where(place[None, :] < incoming[:, None], 1.0, 0.0).astype(jnp.float32)
    outgoing = lax.dynamic_index_in_dim(counts, shard_self, 0, keepdims=False)
    out_live = place[None, :] < outgoing[:, None]
    replica = jnp.concatenate([jnp.zeros((owned,), jnp.bool_), out_live.reshape(-1)])
    sent_first = first_step[owned:].reshape(shards, slots_each, columns)
    sent_second = second_step[owned:].reshape(shards, slots_each, columns)
    got_first, got_second = (
        lax.all_to_all(
            sent_first.astype(jnp.bfloat16), "table", split_axis=0, concat_axis=0, tiled=True
        ).astype(sent_first.dtype),
        lax.all_to_all(
            sent_second.astype(jnp.bfloat16), "table", split_axis=0, concat_axis=0, tiled=True
        ).astype(sent_second.dtype),
    )
    add_first = jax.ops.segment_sum(
        (got_first * in_live[..., None]).reshape(-1, columns), in_targets, num_segments=hot_rows
    )
    add_second = jax.ops.segment_sum(
        (got_second * in_live[..., None]).reshape(-1, columns), in_targets, num_segments=hot_rows
    )
    tally = jax.ops.segment_sum(in_live.reshape(-1), in_targets, num_segments=hot_rows)
    scale = 1.0 / (1.0 + tally)
    new_first = jnp.where(replica[:, None], 0.0, (first_step + add_first) * scale[:, None])
    new_second = jnp.where(replica[:, None], 0.0, (second_step + add_second) * scale[:, None])
    return (new_first, new_second, replica)


def body(
    token_slot,
    seg_ids,
    req_rows,
    cotangent,
    uvqk_weight,
    table,
    first_moment,
    second_moment,
    dup_count,
    dup_target,
):
    shards = lax.axis_size("table")
    shard_self = lax.axis_index("table")
    hot_rows, width = table.shape
    weight = lax.all_gather(uvqk_weight, "dp", axis=0, tiled=True)
    total = jnp.zeros((hot_rows, width), jnp.float32)
    for micro in range(MICRO):
        held = lax.all_to_all(req_rows[micro], "table", split_axis=0, concat_axis=0, tiled=True)
        found = table[held]
        returned = lax.all_to_all(found, "table", split_axis=0, concat_axis=0, tiled=True)
        fetched, held = (returned, held)
        slots = token_slot[micro, 0]
        inputs = fetched.reshape(-1, width)[slots].astype(jnp.float32)
        segment = seg_ids[micro, 0]
        _, pullback = jax.vjp(lambda given: hstu_block(given, weight, segment, HEADS), inputs)
        grad_inputs = pullback(cotangent[micro].astype(jnp.float32))[0]
        slot_grad = jax.ops.segment_sum(
            grad_inputs, slots, num_segments=fetched.shape[0] * fetched.shape[1]
        )
        arrived = lax.all_to_all(
            slot_grad.reshape(shards, -1, width), "table", split_axis=0, concat_axis=0, tiled=True
        )
        owner_grad = jax.ops.segment_sum(
            arrived.reshape(-1, width), held.reshape(-1), num_segments=hot_rows
        )
        total = total + lax.psum(owner_grad, "dp")
    new_first, new_second, replica = consolidate(
        total, first_moment, second_moment, dup_count, dup_target, shard_self, shards
    )
    update = table.astype(jnp.float32) - learn_rate * new_first / (jnp.sqrt(new_second) + adam_eps)
    new_rows = jnp.where(replica[:, None], 0.0, update).astype(jnp.bfloat16)
    return (new_rows, new_first, new_second)


def solution(mesh):
    placed = (
        P(None, ("dp", "table"), None),
        P(None, ("dp", "table"), None),
        P(None, ("dp", "table"), None),
        P(None, ("dp", "table"), None),
        P("dp", None),
        P("table", None),
        P("table", None),
        P("table", None),
        P(),
        P(),
    )
    return jax.shard_map(
        body,
        mesh=mesh,
        in_specs=placed,
        out_specs=(P("table", None), P("table", None), P("table", None)),
        check_vma=False,
    )
```

profile of v0, /device:TPU:1, one launch (start us, length us, event | category | flops | bytes accessed | tf_op | source)
XLA Modules:
  0.0 524.4 jit_solution(1699242697589699467)
XLA Ops:
  9.2 10.1 %all-to-all-start = ((s32[8,1,16]{2,1,0:T(1,128)}), s32[8,1,16]{2,1,0:T(1,128)S(1)}, u32[]{:S(2)}, u32[]{:S(2)}) async-start(s32[8,1,16]{2,1,0:T(1,128)} %bitcast.2), calls=%async_computation | async-start | bytes 8192 | tf_op jit(solution)/shard_map/all_to_all | solution.py:107
  21.6 2.2 all-to-all-done
  23.8 3.9 all-to-all-start.3
  27.8 2.7 gather_fusion
  30.6 1.7 all-to-all-done.3
  32.2 4.0 all-to-all-start.1
  36.4 1.6 gather_fusion.2
  37.9 4.9 all-to-all-done.1
  42.8 4.4 all-to-all-start.4
  48.5 5.2 all-to-all-done.4
  55.7 99.1 %all-gather.2.cloned.1.call-done = bf16[1024,2048]{1,0:T(8,128)(2,1)} async-done(((bf16[16,2048]{1,0:T(8,128)(2,1)}), bf16[1024,2048]{1,0:T(8,128)(2,1)}) %all-gather.2.cloned.1.call-update) | async-done | bytes 4194320 | tf_op jit(solution)/shard_map/all_gather | solution.py:104
  154.8 5.7 %fusion.143 = (bf16[256,2048]{1,0:T(8,128)(2,1)S(1)}, f32[256,2048]{1,0:T(8,128)}, f32[256,2048]{1,0:T(8,128)}) fusion(bf16[1024,2048]{1,0:T(8,128)(2,1)} %all-gather.2.cloned.1.call-done, bf16[256,1024]{1,0:T(8,128)(2,1)S(1)} %gather_fusion.1, f32[256]{0:T(256)S(1)} %fusion.126, f32[256]{0:T(256)S(1)} %broadcast_multiply_fusion.3), kind=kOutput, calls=%fused_computation.231 | convolution fusion | flops 1077411840 | bytes 9963520 | tf_op jit(solution)/shard_map/jvp()/dot_general | solution.py:26
  160.9 1.6 divide_convert_fusion.1
  163.8 3.5 fusion.141
  168.4 1.5 divide_convert_fusion
  172.8 2.7 fusion.139
  176.4 2.0 fusion.57
  180.1 2.0 fusion.54
  184.6 5.0 fusion.51
  190.0 3.8 scatter_custom_fusion.2
  193.8 13.0 %all-to-all-start.5 = ((f32[8,16,1024]{2,1,0:T(8,128)}), f32[8,16,1024]{2,1,0:T(8,128)S(1)}, u32[]{:S(2)}, u32[]{:S(2)}) async-start(f32[8,16,1024]{2,1,0:T(8,128)} %bitcast.47), calls=%async_computation.5 | async-start | bytes 1048576 | tf_op jit(solution)/shard_map/all_to_all | solution.py:119
  207.3 4.5 fusion.48
  212.3 3.7 scatter_custom_fusion
  217.1 4.6 all-to-all-start.2
  224.4 2.2 scatter_custom_fusion.3
  226.6 4.6 all-to-all-done.2
  231.2 1.7 scatter_custom_fusion.1
  235.2 247.8 %all-reduce.11.cloned.1.call-done = f32[128,1024]{1,0:T(8,128)} async-done(((f32[128,1024]{1,0:T(8,128)}), f32[128,1024]{1,0:T(8,128)}) %all-reduce.11.cloned.1.call-update) | async-done | bytes 524304 | tf_op jit(solution)/shard_map/psum | solution.py:125
  485.0 15.0 %all-to-all-start.7 = ((bf16[8,8,1024]{2,1,0:T(8,128)(2,1)}), bf16[8,8,1024]{2,1,0:T(8,128)(2,1)S(1)}, u32[]{:S(2)}, u32[]{:S(2)}) async-start(bf16[8,8,1024]{2,1,0:T(8,128)(2,1)} %fusion.122), calls=%async_computation.7 | async-start | bytes 262144 | tf_op jit(solution)/shard_map/all_to_all | solution.py:72
  500.6 4.6 all-to-all-done.7
  505.2 4.1 all-to-all-start.6
  510.8 3.9 all-to-all-done.6
  (149 shorter events, 32.3 us)
Async XLA Ops:
  7.2 29.2 %copy-start = (bf16[128,1024]{1,0:T(8,128)(2,1)S(1)}, bf16[128,1024]{1,0:T(8,128)(2,1)}, u32[]{:S(2)}) copy-start(bf16[128,1024]{1,0:T(8,128)(2,1)} %param.15) | copy-start | bytes 786436
  7.2 147.6 %all-gather.2.cloned.1.call-start = ((), (), s32[]{:S(2)}) async-start(), calls=%async_computation.8 | async-start | bytes 4259840 | tf_op jit(solution)/shard_map/all_gather | solution.py:104
  9.2 14.6 %all-to-all-start = ((s32[8,1,16]{2,1,0:T(1,128)}), s32[8,1,16]{2,1,0:T(1,128)S(1)}, u32[]{:S(2)}, u32[]{:S(2)}) async-start(s32[8,1,16]{2,1,0:T(1,128)} %bitcast.2), calls=%async_computation | async-start | bytes 8192 | tf_op jit(solution)/shard_map/all_to_all | solution.py:107
  21.6 139.3 %copy-start.22 = (f32[256,256]{1,0:T(8,128)}, f32[256,256]{1,0:T(8,128)S(1)}, u32[]{:S(2)}) copy-start(f32[256,256]{1,0:T(8,128)S(1)} %get-tuple-element.43) | copy-start | bytes 786436
  23.8 8.4 %all-to-all-start.3 = ((s32[8,1,16]{2,1,0:T(1,128)}), s32[8,1,16]{2,1,0:T(1,128)S(1)}, u32[]{:S(2)}, u32[]{:S(2)}) async-start(s32[8,1,16]{2,1,0:T(1,128)} %bitcast.26), calls=%async_computation.3 | async-start | bytes 8192 | tf_op jit(solution)/shard_map/all_to_all | solution.py:107
  32.2 10.5 %all-to-all-start.1 = ((bf16[8,16,1024]{2,1,0:T(8,128)(2,1)}), bf16[8,16,1024]{2,1,0:T(8,128)(2,1)S(1)}, u32[]{:S(2)}, u32[]{:S(2)}) async-start(bf16[8,16,1024]{2,1,0:T(8,128)(2,1)} %bitcast.6), calls=%async_computation.1 | async-start | bytes 524288 | tf_op jit(solution)/shard_map/all_to_all | solution.py:109
  42.8 10.9 %all-to-all-start.4 = ((bf16[8,16,1024]{2,1,0:T(8,128)(2,1)}), bf16[8,16,1024]{2,1,0:T(8,128)(2,1)S(1)}, u32[]{:S(2)}, u32[]{:S(2)}) async-start(bf16[8,16,1024]{2,1,0:T(8,128)(2,1)} %bitcast.30), calls=%async_computation.4 | async-start | bytes 524288 | tf_op jit(solution)/shard_map/all_to_all | solution.py:109
  47.3 121.0 %copy-start.23 = (f32[256,256]{1,0:T(8,128)}, f32[256,256]{1,0:T(8,128)S(1)}, u32[]{:S(2)}) copy-start(f32[256,256]{1,0:T(8,128)S(1)} %get-tuple-element.41) | copy-start | bytes 786436
  160.6 6.7 %copy-start.16 = (bf16[32,4,8,128]{3,2,1,0:T(8,128)(2,1)}, bf16[32,4,8,128]{3,2,1,0:T(8,128)(2,1)S(1)}, u32[]{:S(2)}) copy-start(bf16[32,4,8,128]{3,2,1,0:T(8,128)(2,1)S(1)} %get-tuple-element.21) | copy-start | bytes 786436
  160.7 1.8 copy-start.6
  160.9 1.7 copy-start.8
  160.9 2.9 copy-start.26
  168.2 1.7 copy-start.10
  168.3 1.6 copy-start.12
  168.3 1.6 copy-start.17
  169.9 1.3 copy-start.1
  176.4 2.1 copy-start.11
  176.4 2.3 copy-start.13
  178.5 1.0 copy-start.5
  178.5 1.1 copy-start.15
  180.1 2.1 copy-start.7
  180.1 2.3 copy-start.9
  190.0 17.3 %copy-start.20 = (f32[256,512]{1,0:T(8,128)S(1)}, f32[256,512]{1,0:T(8,128)}, u32[]{:S(2)}) copy-start(f32[256,512]{1,0:T(8,128)} %get-tuple-element.26) | copy-start | bytes 1572868
  193.8 22.5 %all-to-all-start.5 = ((f32[8,16,1024]{2,1,0:T(8,128)}), f32[8,16,1024]{2,1,0:T(8,128)S(1)}, u32[]{:S(2)}, u32[]{:S(2)}) async-start(f32[8,16,1024]{2,1,0:T(8,128)} %bitcast.47), calls=%async_computation.5 | async-start | bytes 1048576 | tf_op jit(solution)/shard_map/all_to_all | solution.py:119
  211.8 9.9 %copy-start.25 = (s32[64]{0:T(128)S(1)}, s32[64]{0:T(128)}, u32[]{:S(2)}) copy-start(s32[64]{0:T(128)} %param.18) | copy-start | bytes 772
  211.8 10.0 %copy-start.24 = (s32[64,8]{0,1:T(8,128)S(1)}, s32[64,8]{0,1:T(8,128)}, u32[]{:S(2)}) copy-start(s32[64,8]{0,1:T(8,128)} %param.19) | copy-start | bytes 6148
  217.1 266.0 %copy-start.18 = (f32[128,1024]{1,0:T(8,128)S(1)}, f32[128,1024]{1,0:T(8,128)}, u32[]{:S(2)}) copy-start(f32[128,1024]{1,0:T(8,128)} %param.17) | copy-start | bytes 1572868
  217.1 266.0 %copy-start.19 = (f32[128,1024]{1,0:T(8,128)S(1)}, f32[128,1024]{1,0:T(8,128)}, u32[]{:S(2)}) copy-start(f32[128,1024]{1,0:T(8,128)} %param.16) | copy-start | bytes 1572868
  217.1 14.1 %all-to-all-start.2 = ((f32[8,16,1024]{2,1,0:T(8,128)}), f32[8,16,1024]{2,1,0:T(8,128)S(1)}, u32[]{:S(2)}, u32[]{:S(2)}) async-start(f32[8,16,1024]{2,1,0:T(8,128)} %bitcast.23), calls=%async_computation.2 | async-start | bytes 1048576 | tf_op jit(solution)/shard_map/all_to_all | solution.py:119
  221.7 261.3 %all-reduce.11.cloned.1.call-start = ((), (), s32[]{:S(2)}) async-start(), calls=%async_computation.9 | async-start | bytes 1048576 | tf_op jit(solution)/shard_map/psum | solution.py:125
  485.0 20.2 %all-to-all-start.7 = ((bf16[8,8,1024]{2,1,0:T(8,128)(2,1)}), bf16[8,8,1024]{2,1,0:T(8,128)(2,1)S(1)}, u32[]{:S(2)}, u32[]{:S(2)}) async-start(bf16[8,8,1024]{2,1,0:T(8,128)(2,1)} %fusion.122), calls=%async_computation.7 | async-start | bytes 262144 | tf_op jit(solution)/shard_map/all_to_all | solution.py:72
  505.2 9.4 %all-to-all-start.6 = ((bf16[8,8,1024]{2,1,0:T(8,128)(2,1)}), bf16[8,8,1024]{2,1,0:T(8,128)(2,1)S(1)}, u32[]{:S(2)}, u32[]{:S(2)}) async-start(bf16[8,8,1024]{2,1,0:T(8,128)(2,1)} %fusion.121), calls=%async_computation.6 | async-start | bytes 262144 | tf_op jit(solution)/shard_map/all_to_all | solution.py:69
  (5 other events, 4.2 us)
Sparse Core Ops, SparseCore 0:
  11.0 143.7 all-gather.1
  234.0 249.0 all-reduce.10
where the time goes:
time: 526 us; the launch traced here: 524 us
  waiting for transfers between devices  375 us (71%)
  starting transfers between devices  59.2 us (11%)
  matrix products  28.2 us (5%)
  other arithmetic  27.8 us (5%)
  local copies, waits for them, and re-layouts  19.7 us (4%)
  between operations  14.6 us (3%)
    psum x1, waiting for transfers between devices, body(): total = total + lax.psum(owner_grad, 'dp')  248 us
    all_gather x1, waiting for transfers between devices, body(): weight = lax.all_gather(uvqk_weight, 'dp', axis=0, tiled=True)  99.1 us
    dot_general x4, matrix products, hstu_block(): jnp.dot(normed, weight, preferred_element_type=jnp.float32)  18.8 us
    all_to_all x2, starting transfers between devices, body(): lax.all_to_all(slot_grad.reshape(shards, -1, width), 'table', split_axis=...  17.7 us
    all_to_all x1, starting transfers between devices, consolidate(): lax.all_to_all(sent_second.astype(jnp.bfloat16), 'table', split_axis=0, c...  15 us
    all_to_all x2, starting transfers between devices, body(): lax.all_to_all(req_rows[micro], 'table', split_axis=0, concat_axis=0, til...  14 us
  transfers between devices with their start and end apart: 10, of which 10 were waited for; matrix products, arithmetic and copies ran while one was open for 6% of the time, Pallas kernels for 0%

commit v1 on v0

v1 whole, which is shorter than its diff:
```python
import functools

import jax
import jax.numpy as jnp
from jax import lax
from jax.experimental import pallas as pl
from jax.experimental.pallas import tpu as pltpu
from jax.sharding import PartitionSpec as P

MESH = pl.DeviceIdType.MESH
HEADS = 4
MICRO = 2
NX = 4
NY = 4
SHARDS = 8
CAP = 16
DCAP = 8

beta_one = 0.9
beta_two = 0.999
learn_rate = 0.1
adam_eps = 1e-08
norm_eps = 1e-05


def dot(a, b, dims=((1,), (0,))):
    return lax.dot_general(a, b, (dims, ((), ())), preferred_element_type=jnp.float32)


def place():
    dp = lax.axis_index("dp")
    shard = lax.axis_index("table")
    return dp // NY, dp % NY, shard // 2, shard % 2, dp, shard


def greet(peers):
    barrier = pltpu.get_barrier_semaphore()
    for peer in peers:
        pl.semaphore_signal(barrier, inc=1, device_id=peer, device_id_type=MESH)
    pl.semaphore_wait(barrier, len(peers))


def remote(src, dst, send, recv, peer):
    return pltpu.make_async_remote_copy(
        src_ref=src, dst_ref=dst, send_sem=send, recv_sem=recv, device_id=peer, device_id_type=MESH
    )


def slot_rows(held_ref, group):
    rows = held_ref[4 * group]
    for peer in range(1, 4):
        rows = jnp.maximum(rows, held_ref[4 * group + peer])
    number = lax.broadcasted_iota(jnp.int32, (128, 128), 0)
    return jnp.where(number == rows[0:1], 1.0, 0.0).astype(jnp.bfloat16)


def normalise(values):
    center = jnp.mean(values, axis=-1, keepdims=True)
    shifted = values - center
    spread = jnp.mean(shifted * shifted, axis=-1, keepdims=True)
    factor = lax.rsqrt(spread + norm_eps)
    return shifted * factor, factor


def normalise_back(grad, normed, factor):
    grad_mean = jnp.mean(grad, axis=-1, keepdims=True)
    along = jnp.mean(grad * normed, axis=-1, keepdims=True)
    return factor * (grad - grad_mean - normed * along)


def sigmoid(values):
    return 0.5 * jnp.tanh(0.5 * values) + 0.5


def whole_kernel(
    nz,
    req_hbm,
    slot_hbm,
    seg_hbm,
    tally_hbm,
    target_hbm,
    table_hbm,
    w_hbm,
    cot_hbm,
    first_hbm,
    second_hbm,
    first_out,
    second_out,
    req_ref,
    slot_ref,
    seg_ref,
    tally_ref,
    target_ref,
    asked,
    held,
    table_ref,
    wout,
    cot_ref,
    first_ref,
    second_ref,
    found,
    fetched,
    slope,
    flow,
    attn,
    attn_slope,
    mixed,
    back,
    grads,
    arrived,
    y_send,
    y_got,
    z_send,
    z_got,
    total,
    mom_send,
    mom_got,
    rep_send,
    rep_got,
    local_s,
    req_s,
    req_r,
    fnd_s,
    fnd_r,
    z_s,
    z_r,
    ring_s,
    ring_r,
    core_s,
    core_r,
    a_s,
    a_r,
    ry_s,
    ry_r,
    rz_s,
    rz_r,
    gz_s,
    gz_r,
    gy_s,
    gy_r,
    m_s,
    m_r,
    r_s,
    r_r,
):
    z, y, x, core, dp, shard = place()
    other = 1 - core
    half = nz // 2
    columns = table_ref.shape[1]
    blocks = columns // 128
    f32, bf16 = jnp.float32, jnp.bfloat16

    def table_peer(k):
        return lax.rem(shard + k, SHARDS)

    def z_peer(k):
        return lax.rem(z + k, nz)

    def y_peer(k):
        return lax.rem(y + k, NY)

    def along_y(k):
        return (z * NY + y_peer(k), shard)

    def along_x(k):
        return (dp, lax.rem(x + k, NX) * 2 + core)

    across_table = (4, 3, 5, 2, 6, 1, 7)
    across_z = [nz // 2]
    for k in range(nz // 2 - 1, 0, -1):
        across_z += [k, nz - k]
    across_y = (2, 1, 3)

    local = [(req_hbm, req_ref)]
    for g in range(2):
        part = pl.ds(pl.multiple_of(shard * 256 + g * 128, 128), 128)
        local.append((w_hbm.at[:, part], wout.at[x, core, g, z, y]))
    local += [
        (table_hbm, table_ref),
        (cot_hbm, cot_ref),
        (first_hbm, first_ref),
        (second_hbm, second_ref),
        (slot_hbm, slot_ref),
        (seg_hbm, seg_ref),
        (tally_hbm, tally_ref),
        (target_hbm, target_ref),
    ]
    local = [pltpu.make_async_copy(a, b, local_s.at[i]) for i, (a, b) in enumerate(local)]
    for copy in local:
        copy.start()

    local[0].wait()
    lane = lax.broadcasted_iota(jnp.int32, (CAP, 128), 1) % 32
    deep = lax.broadcasted_iota(jnp.int32, (CAP, 128), 0)
    wide = jnp.zeros((SHARDS, 128), f32)
    for m in range(MICRO):
        spot = jnp.where(lane == deep + m * CAP, 1.0, 0.0).astype(bf16)
        wide = wide + dot(req_ref[m].astype(f32).astype(bf16), spot)
    mine = lax.broadcasted_iota(jnp.int32, (SHARDS, 128), 1) // 32 == lax.rem(shard, 4)
    wide = jnp.where(mine, wide.astype(jnp.int32), -1)
    for p in range(SHARDS):
        asked[p] = jnp.broadcast_to(wide[p : p + 1], (8, 128))

    greet(
        [(dp, table_peer(k)) for k in range(1, SHARDS)]
        + [(z_peer(k) * NY + y, shard) for k in range(1, nz)]
        + [along_y(k) for k in range(1, NY)]
    )

    started = []

    def start(copy):
        copy.start()
        started.append(copy)
        return copy

    for k in across_table:
        p = table_peer(k)
        start(remote(asked.at[p], held.at[shard], req_s.at[k], req_r.at[shard], (dp, p)))
    held[shard] = asked[shard]

    local[1].wait()
    local[2].wait()
    for k in across_z:
        q = z_peer(k)
        block = wout.at[x, core, :, z, y]
        start(remote(block, block, z_s.at[k], z_r.at[z], (q * NY + y, shard)))

    local[3].wait()
    for k in reversed(across_table):
        p = table_peer(k)
        remote(asked.at[p], held.at[p], req_s.at[k], req_r.at[p], (dp, p)).wait_recv()
    for group in range(2):
        rows = dot(slot_rows(held, group), table_ref[...], ((0,), (0,)))
        found[4 * group : 4 * group + 4] = rows.astype(bf16).reshape(4, MICRO, CAP, columns)
    for k in across_table:
        p = table_peer(k)
        start(remote(found.at[p], fetched.at[shard], fnd_s.at[k], fnd_r.at[shard], (dp, p)))
    fetched[shard] = found[shard]

    for k in reversed(across_z):
        q = z_peer(k)
        block = wout.at[x, core, :, q, y]
        remote(block, block, z_s.at[k], z_r.at[q], (q * NY + y, shard)).wait_recv()

    whole, low, high = pl.ds(0, nz), pl.ds(0, half), pl.ds(half, half)
    views = (
        lambda i, zs: wout.at[x, core, 0, zs, i],
        lambda i, zs: wout.at[i, core, 1, zs, y],
        lambda i, zs: wout.at[i, core, 0, zs],
        lambda i, zs: wout.at[:, core, 1, zs, i],
    )
    spots = (y, x, x, y)
    steps = (along_y, along_x, along_x, along_y)

    def link(ring, which, offset, zs, to):
        block = views[ring](lax.rem(spots[ring] + offset, 4), zs)
        return remote(
            block, block, ring_s.at[ring, which], ring_r.at[ring, which], steps[ring](to)
        )

    def ring_first(ring):
        start(link(ring, 0, 0, whole, 1))
        start(link(ring, 1, 0, whole, 3))

    def ring_second(ring):
        link(ring, 0, 3, whole, 1).wait_recv()
        start(link(ring, 2, 3, low, 1))
        link(ring, 1, 1, whole, 3).wait_recv()
        start(link(ring, 3, 1, high, 3))

    def ring_third(ring):
        link(ring, 2, 2, low, 1).wait_recv()
        link(ring, 3, 2, high, 3).wait_recv()

    def across(ring, offset, mine=True):
        i = lax.rem(spots[ring] + offset, 4)
        c = core if mine else other
        block = wout.at[i, c, 0] if ring == 2 else wout.at[:, c, 1, :, i]
        s = (ring - 2) * 4 + offset
        return remote(block, block, core_s.at[s], core_r.at[s], (dp, x * 2 + other))

    for ring in (0, 1):
        ring_first(ring)
    for ring in (0, 1):
        ring_second(ring)
    for ring in (0, 1):
        ring_third(ring)
    for ring in (2, 3):
        ring_first(ring)
        start(across(ring, 0))

    for k in reversed(across_table):
        p = table_peer(k)
        remote(found.at[p], fetched.at[p], fnd_s.at[k], fnd_r.at[p], (dp, p)).wait_recv()
    for copy in local[7:]:
        copy.wait()
    count = seg_ref.shape[2]
    slots = SHARDS * CAP
    collect, expand, share = [], [], []
    number = lax.broadcasted_iota(jnp.int32, (slots, count), 0)
    user = lax.broadcasted_iota(jnp.int32, (8, count), 0)
    causal = lax.broadcasted_iota(jnp.int32, (count, count), 0) >= lax.broadcasted_iota(
        jnp.int32, (count, count), 1
    )
    for m in range(MICRO):
        hot = jnp.where(number == slot_ref[m], 1.0, 0.0)
        collect.append(hot.astype(bf16))
        expand.append(jnp.transpose(hot).astype(bf16))
        belongs = jnp.where(user == seg_ref[m], 1.0, 0.0).astype(bf16)
        same = dot(belongs, belongs, ((0,), (0,)))
        history = jnp.sum(same, axis=1, keepdims=True)
        share.append(jnp.where(causal, same, 0.0) / history)
    rows = jnp.concatenate(
        [fetched[:, m].reshape(slots, columns) for m in range(MICRO)], axis=0
    ).astype(f32)
    normed, factor = normalise(rows)
    given = normed.astype(bf16)

    i32 = jnp.int32
    live = lax.broadcasted_iota(i32, (DCAP, 64), 0) < tally_ref[...]
    aims = jnp.where(live, target_ref[...] + 1, 0).astype(f32).astype(bf16)
    lane = lax.broadcasted_iota(i32, (64, 64), 1)
    deep = lax.broadcasted_iota(i32, (64, 64), 0)
    here = jnp.where(deep == (lane // DCAP) * SHARDS + shard, 1.0, 0.0).astype(bf16)
    aims = dot(aims, here)
    lane = lax.broadcasted_iota(i32, (DCAP, 64), 1) % DCAP
    deep = lax.broadcasted_iota(i32, (DCAP, 64), 0)
    aims = jnp.sum(jnp.where(lane == deep, aims, 0.0), axis=0, keepdims=True).astype(i32) - 1
    number = lax.broadcasted_iota(i32, (128, 64), 0)
    pick = jnp.where(number == aims, 1.0, 0.0)
    tally = jnp.sum(pick, axis=1, keepdims=True)
    pick = pick.astype(bf16)
    lane = lax.broadcasted_iota(i32, (64, 64), 1)
    deep = lax.broadcasted_iota(i32, (64, 64), 0)
    limit = jnp.where(lane == shard * SHARDS + deep // DCAP, tally_ref[...].astype(f32), 0.0)
    limit = jnp.sum(limit, axis=1, keepdims=True)
    row = (lax.broadcasted_iota(i32, (64, 1), 0) % DCAP).astype(f32)
    scale = 1.0 / (1.0 + tally)
    scale = jnp.concatenate([scale[:64], jnp.where(row < limit, 0.0, scale[64:])], axis=0)

    for ring in (2, 3):
        ring_second(ring)
        start(across(ring, 3))
        start(across(ring, 1))
    for ring in (2, 3):
        ring_third(ring)
        start(across(ring, 2))

    for copy in local[4:7]:
        copy.wait()
    for p in range(SHARDS):
        line = slice(64 + DCAP * p, 64 + DCAP * p + DCAP)
        mom_send[p] = jnp.concatenate([first_ref[line], second_ref[line]], axis=0).astype(bf16)
    for ring in (2, 3):
        for offset in (0, 3, 1, 2):
            across(ring, offset, mine=False).wait_recv()
    for k in across_table:
        p = table_peer(k)
        start(remote(mom_send.at[p], mom_got.at[shard], m_s.at[k], m_r.at[shard], (dp, p)))
    mom_got[shard] = mom_send[shard]

    width = 512
    head = width // HEADS

    def weight(i):
        sides = [wout[i // 2, i % 2, g].reshape(columns, 128) for g in range(2)]
        return jnp.concatenate(sides, axis=1)

    for i in range(8):
        flat = dot(given, weight(i))
        sig = sigmoid(flat)
        value = flat * sig
        slope[:, 256 * i : 256 * i + 256] = sig * (1.0 + flat * (1.0 - sig))
        top = value.astype(bf16)
        for m in range(MICRO):
            span = slice(m * count, (m + 1) * count)
            part = slice(m * slots, (m + 1) * slots)
            spread = dot(expand[m], top[part])
            flow[span, 256 * i : 256 * i + 256] = spread.astype(bf16)

    def slot_send(piece, src, to, k, p):
        m = min(piece, 1)
        over = slice(None) if piece == 0 else pl.ds((piece - 1) * columns // 2, columns // 2)
        return remote(
            grads.at[src, m, :, over],
            arrived.at[to, m, :, over],
            a_s.at[piece, k],
            a_r.at[piece, to],
            (dp, p),
        )

    factor_scale = head ** (-0.5)
    for m in range(MICRO):
        span = slice(m * count, (m + 1) * count)
        part = slice(m * slots, (m + 1) * slots)
        for h in range(HEADS):
            values = flow[span, width + h * head : width + (h + 1) * head]
            queries = flow[span, 2 * width + h * head : 2 * width + (h + 1) * head]
            keys = flow[span, 3 * width + h * head : 3 * width + (h + 1) * head]
            scores = dot(queries, keys, ((1,), (1,))) * factor_scale
            sig = sigmoid(scores)
            shared = share[m] * sig
            weights = (scores * shared).astype(bf16)
            attn[h] = weights
            attn_slope[h] = shared * (1.0 + scores * (1.0 - sig)) * factor_scale
            mixed[:, h * head : (h + 1) * head] = dot(weights, values)
        level, spread = normalise(mixed[...])
        upstream = cot_ref[m].astype(f32)
        back[:, :width] = (upstream * level).astype(bf16)
        grad_mixed = normalise_back(
            upstream * flow[span, :width].astype(f32), level, spread
        ).astype(bf16)
        for h in range(HEADS):
            values = flow[span, width + h * head : width + (h + 1) * head]
            queries = flow[span, 2 * width + h * head : 2 * width + (h + 1) * head]
            keys = flow[span, 3 * width + h * head : 3 * width + (h + 1) * head]
            grad_out = grad_mixed[:, h * head : (h + 1) * head]
            grad_attn = dot(grad_out, values, ((1,), (1,))).astype(bf16)
            grad_scores = (grad_attn.astype(f32) * attn_slope[h]).astype(bf16)
            at = width + h * head
            back[:, at : at + head] = dot(attn[h], grad_out, ((0,), (0,))).astype(bf16)
            at = 2 * width + h * head
            back[:, at : at + head] = dot(grad_scores, keys).astype(bf16)
            at = 3 * width + h * head
            back[:, at : at + head] = dot(grad_scores, queries, ((0,), (0,))).astype(bf16)
        grad_normed = jnp.zeros((slots, columns), f32)
        for i in range(8):
            side = slice(256 * i, 256 * i + 256)
            grad_flat = (dot(collect[m], back[:, side]) * slope[part, side]).astype(bf16)
            grad_normed = grad_normed + dot(grad_flat, weight(i), ((1,), (1,)))
        grad_normed = grad_normed.astype(bf16).astype(f32)
        slot_grad = normalise_back(grad_normed, normed[part], factor[part]).astype(bf16)
        grads[:, m] = slot_grad.reshape(SHARDS, CAP, columns)
        for piece in ((0,), (1, 2))[m]:
            for k in across_table:
                start(slot_send(piece, table_peer(k), shard, k, table_peer(k)))
    arrived[shard] = grads[shard]

    asks = [slot_rows(held, group) for group in range(2)]
    side = columns // 2
    tiles = nz // 2
    lines = blocks // 2

    def half_sums(h):
        for piece in ((0, 1), (2,))[h]:
            for k in reversed(across_table):
                p = table_peer(k)
                slot_send(piece, p, p, k, p).wait_recv()
        dense = jnp.zeros((128, side), f32)
        for group in range(2):
            came = arrived[4 * group : 4 * group + 4, :, :, h * side : (h + 1) * side]
            dense = dense + dot(asks[group], came.reshape(128, side))
        dense = dense.astype(bf16)
        for part in range(NY):
            for r in range(2):
                for b in range(lines):
                    at = part * 32 + r * 16
                    y_send[part, h * tiles + r * lines + b] = dense[
                        at : at + 16, b * 128 : b * 128 + 128
                    ]

    def half_y(h, q, to, k):
        part = pl.ds(h * tiles, tiles)
        return remote(
            y_send.at[q, part], y_got.at[to, part], ry_s.at[h, k], ry_r.at[h, to], along_y(k)
        )

    def half_z(h, j):
        q = lax.rem(z + j, tiles) + h * tiles
        return remote(z_send.at[q], z_got.at[z], rz_s.at[h, j], rz_r.at[z], (q * NY + y, shard))

    around = [tiles // 2]
    for j in range(tiles // 2 - 1, 0, -1):
        around += [j, tiles - j]

    for h in range(2):
        half_sums(h)
        for k in across_y:
            start(half_y(h, y_peer(k), y, k))
    for h in range(2):
        part = slice(h * tiles, (h + 1) * tiles)
        y_sum = y_send[y, part].astype(f32)
        for k in reversed(across_y):
            q = y_peer(k)
            half_y(h, q, q, k).wait_recv()
            y_sum = y_sum + y_got[q, part].astype(f32)
        z_send[part] = y_sum.astype(bf16)
        for j in around:
            start(half_z(h, j))

        @pl.when(z // tiles != h)
        def _():
            half_z(h, 0).start()

    z_sum = z_send[z].astype(f32)
    for k in reversed(across_z):
        q = z_peer(k)
        remote(z_send.at[q], z_got.at[q], rz_s.at[0, 0], rz_r.at[q], (q * NY + y, shard)).wait_recv()
        z_sum = z_sum + z_got[q].astype(f32)
    total[y, z] = z_sum.astype(bf16)

    for k in across_z:
        q = z_peer(k)
        block = total.at[y, z]
        start(remote(block, block, gz_s.at[k], gz_r.at[z], (q * NY + y, shard)))
    def tile_of(q):
        block = total.at[y, q]
        return remote(block, block, gz_s.at[1], gz_r.at[q], (q * NY + y, shard))

    def out_y(h, q, k):
        block = total.at[q, pl.ds(h * tiles, tiles)]
        return remote(block, block, gy_s.at[h, k], gy_r.at[h, q], along_y(k))

    for h in range(2):
        for j in reversed(around):
            tile_of(lax.rem(z + j, tiles) + h * tiles).wait_recv()

        @pl.when(z // tiles != h)
        def _():
            tile_of(lax.rem(z, tiles) + h * tiles).wait_recv()

        for k in across_y:
            start(out_y(h, y, k))

    for k in reversed(across_table):
        p = table_peer(k)
        remote(mom_send.at[p], mom_got.at[p], m_s.at[k], m_r.at[p], (dp, p)).wait_recv()
    def rep_out(h, src, to, k, p):
        return remote(
            rep_send.at[h, src], rep_got.at[h, to], r_s.at[h, k], r_r.at[h, to], (dp, p)
        )

    for h in range(2):
        for k in reversed(across_y):
            out_y(h, y_peer(k), k).wait_recv()
        grad = [
            jnp.concatenate(
                [total[n // 2, h * tiles + (n % 2) * lines + b] for b in range(lines)], axis=1
            ).astype(f32)
            for n in range(8)
        ]
        for p in range(SHARDS):
            own = grad[4 + p // 2][(p % 2) * 8 : (p % 2) * 8 + 8]
            rep_send[h, p] = jnp.concatenate(
                [own[:, : side // 2], own[:, side // 2 :]], axis=0
            ).astype(bf16)
        for k in across_table:
            p = table_peer(k)
            start(rep_out(h, p, shard, k, p))
        rep_got[h, shard] = rep_send[h, shard]
        over = slice(h * side, (h + 1) * side)
        for n in range(8):
            span = slice(16 * n, 16 * n + 16)
            first_out[span, over] = beta_one * first_ref[span, over] + (1.0 - beta_one) * grad[n]
            second_out[span, over] = beta_two * second_ref[span, over] + (1.0 - beta_two) * (
                grad[n] * grad[n]
            )
    for h in range(2):
        over = slice(h * side, (h + 1) * side)
        for k in reversed(across_table):
            p = table_peer(k)
            rep_out(h, p, p, k, p).wait_recv()
        rep_first, rep_second = [], []
        for p in range(SHARDS):
            halves = rep_got[h, p].astype(f32)
            grad = jnp.concatenate([halves[:8], halves[8:]], axis=1)
            moments = mom_got[p, :, over].astype(f32)
            rep_first.append(beta_one * moments[:8] + (1.0 - beta_one) * grad)
            rep_second.append(beta_two * moments[8:] + (1.0 - beta_two) * (grad * grad))
        rep_first = dot(pick, jnp.concatenate(rep_first, axis=0).astype(bf16))
        rep_second = dot(pick, jnp.concatenate(rep_second, axis=0).astype(bf16))
        first_out[:, over] = (first_out[:, over] + rep_first) * scale
        second_out[:, over] = (second_out[:, over] + rep_second) * scale
    for h in range(2):

        @pl.when(z // tiles != h)
        def _():
            half_z(h, 0).wait_send()

    for copy in started:
        copy.wait_send()


def body(
    nz,
    token_slot,
    seg_ids,
    req_rows,
    cotangent,
    uvqk_weight,
    table,
    first_moment,
    second_moment,
    dup_count,
    dup_target,
):
    columns = table.shape[1]
    count = token_slot.shape[2]
    tokens = MICRO * count
    slots = SHARDS * CAP
    vmem = pl.BlockSpec(memory_space=pltpu.VMEM)
    hbm = pl.BlockSpec(memory_space=pl.ANY)
    dma = pltpu.SemaphoreType.DMA
    bf16, f32, i32 = jnp.bfloat16, jnp.float32, jnp.int32

    tiles = 2 * columns // 128
    first, second = pl.pallas_call(
        functools.partial(whole_kernel, nz),
        out_shape=(
            jax.ShapeDtypeStruct(table.shape, f32),
            jax.ShapeDtypeStruct(table.shape, f32),
        ),
        in_specs=[hbm] * 10,
        out_specs=(vmem,) * 2,
        scratch_shapes=[
            pltpu.VMEM(req_rows.shape, i32),
            pltpu.VMEM(token_slot.shape, i32),
            pltpu.VMEM(seg_ids.shape, i32),
            pltpu.VMEM((1, SHARDS * SHARDS), i32),
            pltpu.VMEM((DCAP, SHARDS * SHARDS), i32),
            pltpu.VMEM((SHARDS, 8, 128), i32),
            pltpu.VMEM((SHARDS, 8, 128), i32),
            pltpu.VMEM(table.shape, bf16),
            pltpu.VMEM((NX, 2, 2, nz, NY, 16, 128), bf16),
            pltpu.VMEM((MICRO, count, 512), bf16),
            pltpu.VMEM(table.shape, f32),
            pltpu.VMEM(table.shape, f32),
            pltpu.VMEM((SHARDS, MICRO, CAP, columns), bf16),
            pltpu.VMEM((SHARDS, MICRO, CAP, columns), bf16),
            pltpu.VMEM((MICRO * slots, 2048), f32),
            pltpu.VMEM((tokens, 2048), bf16),
            pltpu.VMEM((HEADS, count, count), bf16),
            pltpu.VMEM((HEADS, count, count), f32),
            pltpu.VMEM((count, 512), f32),
            pltpu.VMEM((count, 2048), bf16),
            pltpu.VMEM((SHARDS, MICRO, CAP, columns), bf16),
            pltpu.VMEM((SHARDS, MICRO, CAP, columns), bf16),
            pltpu.VMEM((NY, tiles, 16, 128), bf16),
            pltpu.VMEM((NY, tiles, 16, 128), bf16),
            pltpu.VMEM((tiles, 16, 128), bf16),
            pltpu.VMEM((tiles, 16, 128), bf16),
            pltpu.VMEM((NY, tiles, 16, 128), bf16),
            pltpu.VMEM((SHARDS, 16, columns), bf16),
            pltpu.VMEM((SHARDS, 16, columns), bf16),
            pltpu.VMEM((2, SHARDS, 16, columns // 4), bf16),
            pltpu.VMEM((2, SHARDS, 16, columns // 4), bf16),
            dma((11,)),
            dma((SHARDS,)),
            dma((SHARDS,)),
            dma((SHARDS,)),
            dma((SHARDS,)),
            dma((nz,)),
            dma((nz,)),
            dma((4, 4)),
            dma((4, 4)),
            dma((8,)),
            dma((8,)),
            dma((3, SHARDS)),
            dma((3, SHARDS)),
            dma((2, NY)),
            dma((2, NY)),
            dma((2, nz // 2)),
            dma((nz,)),
            dma((nz,)),
            dma((nz,)),
            dma((2, NY)),
            dma((2, NY)),
            dma((SHARDS,)),
            dma((SHARDS,)),
            dma((2, SHARDS)),
            dma((2, SHARDS)),
        ],
        compiler_params=pltpu.CompilerParams(
            collective_id=0, has_side_effects=True, vmem_limit_bytes=63 << 20
        ),
        name="whole",
    )(
        req_rows,
        token_slot,
        seg_ids,
        dup_count[None, :],
        dup_target.T,
        table,
        uvqk_weight,
        cotangent,
        first_moment,
        second_moment,
    )
    keep = second > 0.0
    new_first = jnp.where(keep, first, 0.0)
    new_second = jnp.where(keep, second, 0.0)
    update = table.astype(f32) - learn_rate * new_first / (jnp.sqrt(new_second) + adam_eps)
    return (jnp.where(keep, update, 0.0).astype(bf16), new_first, new_second)


def solution(mesh):
    placed = (
        P(None, ("dp", "table"), None),
        P(None, ("dp", "table"), None),
        P(None, ("dp", "table"), None),
        P(None, ("dp", "table"), None),
        P("dp", None),
        P("table", None),
        P("table", None),
        P("table", None),
        P(),
        P(),
    )
    return jax.shard_map(
        functools.partial(body, mesh.shape["dp"] // NY),
        mesh=mesh,
        in_specs=placed,
        out_specs=(P("table", None), P("table", None), P("table", None)),
        check_vma=False,
    )
```

time: 526 us -> 98.8 us (0.19)
  waiting for transfers between devices: 375 us -> 0 us
  Pallas kernels: 0 us -> 95.6 us
  starting transfers between devices: 59.2 us -> 0 us
  matrix products: 28.2 us -> 0 us
  other arithmetic: 27.8 us -> 2.46 us
  local copies, waits for them, and re-layouts: 19.7 us -> 0.01 us
  between operations: 14.6 us -> 0.66 us
    psum x1 -> x0, waiting for transfers between devices: 248 us -> none  [body(): total = total + lax.psum(owner_grad, 'dp')]
    all_gather x1 -> x0, waiting for transfers between devices: 99.1 us -> none  [body(): weight = lax.all_gather(uvqk_weight, 'dp', axis=0, tiled=True)]
    pallas_call x0 -> x1, Pallas kernels: none -> 95.6 us  [body(): pl.pallas_call(functools.partial(whole_kernel, nz), out_shape=(jax.ShapeD...]
    all_to_all x8 -> x0, starting transfers between devices: 59.1 us -> none  [the longest x2 17.7 us: body(): lax.all_to_all(slot_grad.reshape(shards, -1, width), 'table', split_axis=...]
    dot_general x16 -> x0, matrix products: 28.2 us -> none  [the longest x4 18.8 us: hstu_block(): jnp.dot(normed, weight, preferred_element_type=jnp.float32)]
    all_to_all x8 -> x0, waiting for transfers between devices: 27.3 us -> none  [the longest x2 10 us: body(): lax.all_to_all(found, 'table', split_axis=0, concat_axis=0, tiled=True)]
    scatter-add x7 -> x0, other arithmetic: 15.3 us -> none  [the longest x2 7.5 us: body(): jax.ops.segment_sum(grad_inputs, slots, num_segments=fetched.shape[0] * f...]
    gather x4 -> x0, local copies, waits for them, and re-layouts: 6.63 us -> none  [the longest x2 4.29 us: body(): found = table[held]]
  transfers between devices with their start and end apart: 10 -> 0, of which waited for: 10 -> 0; matrix products, arithmetic and copies ran while one was open for 6% -> 0% of each run, Pallas kernels for 0% -> 0%
where the time goes in v1:
time: 98.8 us; the launch traced here: 98.7 us
  Pallas kernels  95.6 us (97%)
  other arithmetic  2.46 us (2%)
    pallas_call x1, Pallas kernels, body(): pl.pallas_call(functools.partial(whole_kernel, nz), out_shape=(jax.ShapeD...  95.6 us
    convert_element_type x1, other arithmetic, body(): return (jnp.where(keep, update, 0.0).astype(bf16), new_first, new_second)  2.46 us

profile of v1, /device:TPU:1, one launch (start us, length us, event | category | flops | bytes accessed | tf_op | source)
XLA Modules:
  0.0 98.7 jit_solution(1394795484737894088)
XLA Ops:
  0.6 0.0 copy-start
  0.6 95.6 %whole.1 = (f32[128,1024]{1,0:T(8,128)}, f32[128,1024]{1,0:T(8,128)}) custom-call(s32[2,8,16]{2,1,0:T(8,128)} %req_hbm.1, s32[2,1,256]{2,1,0:T(1,128)} %slot_hbm.1, s32[2,1,256]{2,1,0:T(1,128)} %seg_hbm.1, s32[1,64]{1,0:T(1,128)} %bitcast.3, s32[8,64]{1,0:T(8,128)} %bitcast.2, bf16[128,1024]{1,0:T(8,128)(2,1)} %table_hbm.1, bf16[16,2048]{1,0:T(8,128)(2,1)} %w_hbm.1, ...), custom_call_target="tpu_custom_call" | custom-call | tf_op jit(solution)/shard_map/whole/pallas_call | solution.py:608
  96.2 0.0 copy-done
  96.2 2.5 %select_convert_fusion = (bf16[128,1024]{1,0:T(8,128)(2,1)}, f32[128,1024]{1,0:T(8,128)}, f32[128,1024]{1,0:T(8,128)}) fusion(bf16[128,1024]{1,0:T(8,128)(2,1)S(1)} %copy-done, f32[128,1024]{1,0:T(8,128)} %get-tuple-element.5, f32[128,1024]{1,0:T(8,128)} %get-tuple-element.6), kind=kLoop, calls=%fused_computation | loop fusion | flops 1310720 | bytes 2621440 | tf_op jit(solution)/shard_map/convert_element_type | solution.py:694
Async XLA Ops:
  0.6 95.6 %copy-start = (bf16[128,1024]{1,0:T(8,128)(2,1)S(1)}, bf16[128,1024]{1,0:T(8,128)(2,1)}, u32[]{:S(2)}) copy-start(bf16[128,1024]{1,0:T(8,128)(2,1)} %table_hbm.1) | copy-start | bytes 786436

commit v2 on v1

--- a/solution.py
+++ b/solution.py
@@ -112,6 +112,7 @@
     y_got,
     z_send,
     z_got,
+    far,
     total,
     mom_send,
     mom_got,
@@ -134,6 +135,8 @@
     ry_r,
     rz_s,
     rz_r,
+    fz_s,
+    fz_r,
     gz_s,
     gz_r,
     gy_s,
@@ -214,10 +217,10 @@
         started.append(copy)
         return copy
 
-    for k in across_table:
-        p = table_peer(k)
-        start(remote(asked.at[p], held.at[shard], req_s.at[k], req_r.at[shard], (dp, p)))
-    held[shard] = asked[shard]
+    def drain():
+        for copy in started:
+            copy.wait_send()
+        started.clear()
 
     local[1].wait()
     local[2].wait()
@@ -225,6 +228,11 @@
         q = z_peer(k)
         block = wout.at[x, core, :, z, y]
         start(remote(block, block, z_s.at[k], z_r.at[z], (q * NY + y, shard)))
+
+    for k in across_table:
+        p = table_peer(k)
+        start(remote(asked.at[p], held.at[shard], req_s.at[k], req_r.at[shard], (dp, p)))
+    held[shard] = asked[shard]
 
     local[3].wait()
     for k in reversed(across_table):
@@ -379,15 +387,9 @@
             spread = dot(expand[m], top[part])
             flow[span, 256 * i : 256 * i + 256] = spread.astype(bf16)
 
-    def slot_send(piece, src, to, k, p):
-        m = min(piece, 1)
-        over = slice(None) if piece == 0 else pl.ds((piece - 1) * columns // 2, columns // 2)
+    def slot_send(m, src, to, k, p):
         return remote(
-            grads.at[src, m, :, over],
-            arrived.at[to, m, :, over],
-            a_s.at[piece, k],
-            a_r.at[piece, to],
-            (dp, p),
+            grads.at[src, m], arrived.at[to, m], a_s.at[m, k], a_r.at[m, to], (dp, p)
         )
 
     factor_scale = head ** (-0.5)
@@ -432,154 +434,127 @@
         grad_normed = grad_normed.astype(bf16).astype(f32)
         slot_grad = normalise_back(grad_normed, normed[part], factor[part]).astype(bf16)
         grads[:, m] = slot_grad.reshape(SHARDS, CAP, columns)
-        for piece in ((0,), (1, 2))[m]:
-            for k in across_table:
-                start(slot_send(piece, table_peer(k), shard, k, table_peer(k)))
+        for k in across_table:
+            start(slot_send(m, table_peer(k), shard, k, table_peer(k)))
     arrived[shard] = grads[shard]
 
     asks = [slot_rows(held, group) for group in range(2)]
-    side = columns // 2
-    tiles = nz // 2
-    lines = blocks // 2
-
-    def half_sums(h):
-        for piece in ((0, 1), (2,))[h]:
-            for k in reversed(across_table):
-                p = table_peer(k)
-                slot_send(piece, p, p, k, p).wait_recv()
-        dense = jnp.zeros((128, side), f32)
-        for group in range(2):
-            came = arrived[4 * group : 4 * group + 4, :, :, h * side : (h + 1) * side]
-            dense = dense + dot(asks[group], came.reshape(128, side))
-        dense = dense.astype(bf16)
-        for part in range(NY):
-            for r in range(2):
-                for b in range(lines):
-                    at = part * 32 + r * 16
-                    y_send[part, h * tiles + r * lines + b] = dense[
-                        at : at + 16, b * 128 : b * 128 + 128
-                    ]
-
-    def half_y(h, q, to, k):
-        part = pl.ds(h * tiles, tiles)
-        return remote(
-            y_send.at[q, part], y_got.at[to, part], ry_s.at[h, k], ry_r.at[h, to], along_y(k)
-        )
-
-    def half_z(h, j):
-        q = lax.rem(z + j, tiles) + h * tiles
-        return remote(z_send.at[q], z_got.at[z], rz_s.at[h, j], rz_r.at[z], (q * NY + y, shard))
-
-    around = [tiles // 2]
-    for j in range(tiles // 2 - 1, 0, -1):
-        around += [j, tiles - j]
-
-    for h in range(2):
-        half_sums(h)
-        for k in across_y:
-            start(half_y(h, y_peer(k), y, k))
-    for h in range(2):
-        part = slice(h * tiles, (h + 1) * tiles)
-        y_sum = y_send[y, part].astype(f32)
-        for k in reversed(across_y):
-            q = y_peer(k)
-            half_y(h, q, q, k).wait_recv()
-            y_sum = y_sum + y_got[q, part].astype(f32)
-        z_send[part] = y_sum.astype(bf16)
-        for j in around:
-            start(half_z(h, j))
-
-        @pl.when(z // tiles != h)
-        def _():
-            half_z(h, 0).start()
-
-    z_sum = z_send[z].astype(f32)
-    for k in reversed(across_z):
-        q = z_peer(k)
-        remote(z_send.at[q], z_got.at[q], rz_s.at[0, 0], rz_r.at[q], (q * NY + y, shard)).wait_recv()
-        z_sum = z_sum + z_got[q].astype(f32)
-    total[y, z] = z_sum.astype(bf16)
-
-    for k in across_z:
-        q = z_peer(k)
-        block = total.at[y, z]
-        start(remote(block, block, gz_s.at[k], gz_r.at[z], (q * NY + y, shard)))
-    def tile_of(q):
-        block = total.at[y, q]
-        return remote(block, block, gz_s.at[1], gz_r.at[q], (q * NY + y, shard))
-
-    def out_y(h, q, k):
-        block = total.at[q, pl.ds(h * tiles, tiles)]
-        return remote(block, block, gy_s.at[h, k], gy_r.at[h, q], along_y(k))
-
-    for h in range(2):
-        for j in reversed(around):
-            tile_of(lax.rem(z + j, tiles) + h * tiles).wait_recv()
-
-        @pl.when(z // tiles != h)
-        def _():
-            tile_of(lax.rem(z, tiles) + h * tiles).wait_recv()
-
-        for k in across_y:
-            start(out_y(h, y, k))
-
-    for k in reversed(across_table):
-        p = table_peer(k)
-        remote(mom_send.at[p], mom_got.at[p], m_s.at[k], m_r.at[p], (dp, p)).wait_recv()
-    def rep_out(h, src, to, k, p):
-        return remote(
-            rep_send.at[h, src], rep_got.at[h, to], r_s.at[h, k], r_r.at[h, to], (dp, p)
-        )
-
-    for h in range(2):
-        for k in reversed(across_y):
-            out_y(h, y_peer(k), k).wait_recv()
-        grad = [
-            jnp.concatenate(
-                [total[n // 2, h * tiles + (n % 2) * lines + b] for b in range(lines)], axis=1
-            ).astype(f32)
-            for n in range(8)
-        ]
-        for p in range(SHARDS):
-            own = grad[4 + p // 2][(p % 2) * 8 : (p % 2) * 8 + 8]
-            rep_send[h, p] = jnp.concatenate(
-                [own[:, : side // 2], own[:, side // 2 :]], axis=0
-            ).astype(bf16)
-        for k in across_table:
-            p = table_peer(k)
-            start(rep_out(h, p, shard, k, p))
-        rep_got[h, shard] = rep_send[h, shard]
-        over = slice(h * side, (h + 1) * side)
-        for n in range(8):
-            span = slice(16 * n, 16 * n + 16)
-            first_out[span, over] = beta_one * first_ref[span, over] + (1.0 - beta_one) * grad[n]
-            second_out[span, over] = beta_two * second_ref[span, over] + (1.0 - beta_two) * (
-                grad[n] * grad[n]
-            )
-    for h in range(2):
-        over = slice(h * side, (h + 1) * side)
+    for m in range(MICRO):
         for k in reversed(across_table):
             p = table_peer(k)
-            rep_out(h, p, p, k, p).wait_recv()
-        rep_first, rep_second = [], []
-        for p in range(SHARDS):
-            halves = rep_got[h, p].astype(f32)
-            grad = jnp.concatenate([halves[:8], halves[8:]], axis=1)
-            moments = mom_got[p, :, over].astype(f32)
-            rep_first.append(beta_one * moments[:8] + (1.0 - beta_one) * grad)
-            rep_second.append(beta_two * moments[8:] + (1.0 - beta_two) * (grad * grad))
-        rep_first = dot(pick, jnp.concatenate(rep_first, axis=0).astype(bf16))
-        rep_second = dot(pick, jnp.concatenate(rep_second, axis=0).astype(bf16))
-        first_out[:, over] = (first_out[:, over] + rep_first) * scale
-        second_out[:, over] = (second_out[:, over] + rep_second) * scale
-    for h in range(2):
-
-        @pl.when(z // tiles != h)
-        def _():
-            half_z(h, 0).wait_send()
-
-    for copy in started:
-        copy.wait_send()
+            slot_send(m, p, p, k, p).wait_recv()
+    dense = jnp.zeros((128, columns), f32)
+    for group in range(2):
+        came = arrived[4 * group : 4 * group + 4].reshape(128, columns)
+        dense = dense + dot(asks[group], came)
+    dense = dense.astype(bf16)
+    for part in range(NY):
+        for r in range(2):
+            for b in range(blocks):
+                at = part * 32 + r * 16
+                y_send[part, r * blocks + b] = dense[at : at + 16, b * 128 : b * 128 + 128]
+
+    def sum_y(q, to, k):
+        return remote(y_send.at[q], y_got.at[to], ry_s.at[k], ry_r.at[to], along_y(k))
+
+    for k in across_y:
+        start(sum_y(y_peer(k), y, k))
+    drain()
+    y_sum = y_send[y].astype(f32)
+    for k in reversed(across_y):
+        sum_y(y_peer(k), y_peer(k), k).wait_recv()
+        y_sum = y_sum + y_got[y_peer(k)].astype(f32)
+    z_send[...] = y_sum.astype(bf16)
+
+    quarter = 2 * blocks // 4
+    rank, near, laps = z % 4, z // 4, nz // 4
+
+    def own(i):
+        return pl.ds(i * quarter, quarter)
+
+    def sum_near(q, to, k):
+        peer = (near * 4 + lax.rem(rank + k, 4)) * NY + y
+        return remote(z_send.at[own(q)], z_got.at[to], rz_s.at[k], rz_r.at[to], (peer, shard))
+
+    def sum_far(to, k):
+        peer = (lax.rem(near + k, laps) * 4 + rank) * NY + y
+        return remote(far.at[near], far.at[to], fz_s.at[k], fz_r.at[to], (peer, shard))
+
+    for k in (2, 1, 3):
+        start(sum_near(lax.rem(rank + k, 4), rank, k))
+    z_sum = z_send[own(rank)].astype(f32)
+    for k in (1, 3, 2):
+        q = lax.rem(rank + k, 4)
+        sum_near(q, q, k).wait_recv()
+        z_sum = z_sum + z_got[q].astype(f32)
+    far[near] = z_sum.astype(bf16)
+    for k in range(laps - 1, 0, -1):
+        start(sum_far(near, k))
+    for k in range(1, laps):
+        sum_far(lax.rem(near + k, laps), k).wait_recv()
+    z_sum = far[0].astype(f32)
+    for i in range(1, laps):
+        z_sum = z_sum + far[i].astype(f32)
+    total[y, own(rank)] = z_sum.astype(bf16)
+
+    def out_z(q, k):
+        block = total.at[y, own(q)]
+        peer = z_peer((0, 1, 2, nz - 1)[k]) * NY + y
+        return remote(block, block, gz_s.at[k], gz_r.at[q], (peer, shard))
+
+    for k in (2, 1, 3):
+        start(out_z(rank, k))
+    for k in (1, 3, 2):
+        q = lax.rem(rank + k, 4)
+        out_z(q, k).wait_recv()
+
+    def out_y(q, k):
+        return remote(total.at[q], total.at[q], gy_s.at[k], gy_r.at[q], along_y(k))
+
+    for k in across_y:
+        start(out_y(y, k))
+    for k in reversed(across_table):
+        p = table_peer(k)
+        remote(mom_send.at[p], mom_got.at[p], m_s.at[k], m_r.at[p], (dp, p)).wait_recv()
+    def rep_out(src, to, k, p):
+        return remote(rep_send.at[src], rep_got.at[to], r_s.at[k], r_r.at[to], (dp, p))
+
+    for k in reversed(across_y):
+        out_y(y_peer(k), k).wait_recv()
+    grad = [
+        jnp.concatenate(
+            [total[n // 2, (n % 2) * blocks + b] for b in range(blocks)], axis=1
+        ).astype(f32)
+        for n in range(8)
+    ]
+    for p in range(SHARDS):
+        sent = grad[4 + p // 2][(p % 2) * 8 : (p % 2) * 8 + 8]
+        rep_send[p] = jnp.concatenate(
+            [sent[:, : columns // 2], sent[:, columns // 2 :]], axis=0
+        ).astype(bf16)
+    for k in across_table:
+        p = table_peer(k)
+        start(rep_out(p, shard, k, p))
+    rep_got[shard] = rep_send[shard]
+    for n in range(8):
+        span = slice(16 * n, 16 * n + 16)
+        first_out[span] = beta_one * first_ref[span] + (1.0 - beta_one) * grad[n]
+        second_out[span] = beta_two * second_ref[span] + (1.0 - beta_two) * (grad[n] * grad[n])
+    drain()
+    for k in reversed(across_table):
+        p = table_peer(k)
+        rep_out(p, p, k, p).wait_recv()
+    rep_first, rep_second = [], []
+    for p in range(SHARDS):
+        halves = rep_got[p].astype(f32)
+        grad = jnp.concatenate([halves[:8], halves[8:]], axis=1)
+        moments = mom_got[p].astype(f32)
+        rep_first.append(beta_one * moments[:8] + (1.0 - beta_one) * grad)
+        rep_second.append(beta_two * moments[8:] + (1.0 - beta_two) * (grad * grad))
+    rep_first = dot(pick, jnp.concatenate(rep_first, axis=0).astype(bf16))
+    rep_second = dot(pick, jnp.concatenate(rep_second, axis=0).astype(bf16))
+    first_out[...] = (first_out[...] + rep_first) * scale
+    second_out[...] = (second_out[...] + rep_second) * scale
 
 
 def body(
@@ -639,12 +614,13 @@
             pltpu.VMEM((NY, tiles, 16, 128), bf16),
             pltpu.VMEM((NY, tiles, 16, 128), bf16),
             pltpu.VMEM((tiles, 16, 128), bf16),
-            pltpu.VMEM((tiles, 16, 128), bf16),
+            pltpu.VMEM((4, tiles // 4, 16, 128), bf16),
+            pltpu.VMEM((nz // 4, tiles // 4, 16, 128), bf16),
             pltpu.VMEM((NY, tiles, 16, 128), bf16),
             pltpu.VMEM((SHARDS, 16, columns), bf16),
             pltpu.VMEM((SHARDS, 16, columns), bf16),
-            pltpu.VMEM((2, SHARDS, 16, columns // 4), bf16),
-            pltpu.VMEM((2, SHARDS, 16, columns // 4), bf16),
+            pltpu.VMEM((SHARDS, 16, columns // 2), bf16),
+            pltpu.VMEM((SHARDS, 16, columns // 2), bf16),
             dma((11,)),
             dma((SHARDS,)),
             dma((SHARDS,)),
@@ -656,20 +632,22 @@
             dma((4, 4)),
             dma((8,)),
             dma((8,)),
-            dma((3, SHARDS)),
-            dma((3, SHARDS)),
-            dma((2, NY)),
-            dma((2, NY)),
-            dma((2, nz // 2)),
-            dma((nz,)),
-            dma((nz,)),
-            dma((nz,)),
-            dma((2, NY)),
-            dma((2, NY)),
-            dma((SHARDS,)),
-            dma((SHARDS,)),
-            dma((2, SHARDS)),
-            dma((2, SHARDS)),
+            dma((MICRO, SHARDS)),
+            dma((MICRO, SHARDS)),
+            dma((NY,)),
+            dma((NY,)),
+            dma((4,)),
+            dma((4,)),
+            dma((nz // 4,)),
+            dma((nz // 4,)),
+            dma((4,)),
+            dma((4,)),
+            dma((NY,)),
+            dma((NY,)),
+            dma((SHARDS,)),
+            dma((SHARDS,)),
+            dma((SHARDS,)),
+            dma((SHARDS,)),
         ],
         compiler_params=pltpu.CompilerParams(
             collective_id=0, has_side_effects=True, vmem_limit_bytes=63 << 20

time: 98.8 us -> 100 us (1.012)
  Pallas kernels: 95.6 us -> 96.7 us
    pallas_call x1, Pallas kernels: 95.6 us -> 96.7 us  [body(): pl.pallas_call(functools.partial(whole_kernel, nz), out_shape=(jax.ShapeD...]
where the time goes in v2:
time: 100 us; the launch traced here: 99.8 us
  Pallas kernels  96.7 us (97%)
  other arithmetic  2.46 us (2%)
    pallas_call x1, Pallas kernels, body(): pl.pallas_call(functools.partial(whole_kernel, nz), out_shape=(jax.ShapeD...  96.7 us
    convert_element_type x1, other arithmetic, body(): return (jnp.where(keep, update, 0.0).astype(bf16), new_first, new_second)  2.46 us

profile of v2, /device:TPU:1, one launch (start us, length us, event | category | flops | bytes accessed | tf_op | source)
XLA Modules:
  0.0 99.8 jit_solution(12144120769196356345)
XLA Ops:
  0.6 0.0 copy-start
  0.6 96.7 %whole.1 = (f32[128,1024]{1,0:T(8,128)}, f32[128,1024]{1,0:T(8,128)}) custom-call(s32[2,8,16]{2,1,0:T(8,128)} %req_hbm.1, s32[2,1,256]{2,1,0:T(1,128)} %slot_hbm.1, s32[2,1,256]{2,1,0:T(1,128)} %seg_hbm.1, s32[1,64]{1,0:T(1,128)} %bitcast.3, s32[8,64]{1,0:T(8,128)} %bitcast.2, bf16[128,1024]{1,0:T(8,128)(2,1)} %table_hbm.1, bf16[16,2048]{1,0:T(8,128)(2,1)} %w_hbm.1, ...), custom_call_target="tpu_custom_call" | custom-call | tf_op jit(solution)/shard_map/whole/pallas_call | solution.py:583
  97.3 0.0 copy-done
  97.4 2.5 %select_convert_fusion = (bf16[128,1024]{1,0:T(8,128)(2,1)}, f32[128,1024]{1,0:T(8,128)}, f32[128,1024]{1,0:T(8,128)}) fusion(bf16[128,1024]{1,0:T(8,128)(2,1)S(1)} %copy-done, f32[128,1024]{1,0:T(8,128)} %get-tuple-element.5, f32[128,1024]{1,0:T(8,128)} %get-tuple-element.6), kind=kLoop, calls=%fused_computation | loop fusion | flops 1310720 | bytes 2621440 | tf_op jit(solution)/shard_map/convert_element_type | solution.py:672
Async XLA Ops:
  0.6 96.7 %copy-start = (bf16[128,1024]{1,0:T(8,128)(2,1)S(1)}, bf16[128,1024]{1,0:T(8,128)(2,1)}, u32[]{:S(2)}) copy-start(bf16[128,1024]{1,0:T(8,128)(2,1)} %table_hbm.1) | copy-start | bytes 786436

commit v3 on v1

--- a/solution.py
+++ b/solution.py
@@ -100,6 +100,8 @@
     second_ref,
     found,
     fetched,
+    given_y,
+    sums,
     slope,
     flow,
     attn,
@@ -214,10 +216,10 @@
         started.append(copy)
         return copy
 
-    for k in across_table:
-        p = table_peer(k)
-        start(remote(asked.at[p], held.at[shard], req_s.at[k], req_r.at[shard], (dp, p)))
-    held[shard] = asked[shard]
+    def drain():
+        for copy in started:
+            copy.wait_send()
+        started.clear()
 
     local[1].wait()
     local[2].wait()
@@ -225,6 +227,11 @@
         q = z_peer(k)
         block = wout.at[x, core, :, z, y]
         start(remote(block, block, z_s.at[k], z_r.at[z], (q * NY + y, shard)))
+
+    for k in across_table:
+        p = table_peer(k)
+        start(remote(asked.at[p], held.at[shard], req_s.at[k], req_r.at[shard], (dp, p)))
+    held[shard] = asked[shard]
 
     local[3].wait()
     for k in reversed(across_table):
@@ -316,6 +323,61 @@
     ).astype(f32)
     normed, factor = normalise(rows)
     given = normed.astype(bf16)
+    lane = lax.broadcasted_iota(jnp.int32, (1, columns), 1)
+    deep = lax.broadcasted_iota(jnp.int32, (columns, 256), 0)
+    for i in range(NY):
+        j = lane[:, 256 * i : 256 * i + 256]
+        origin = ((j // 16) % nz) * (NY * 16) + (j // (16 * nz)) * 16 + j % 16
+        order = jnp.where(deep == origin, 1.0, 0.0).astype(bf16)
+        given_y[:, 256 * i : 256 * i + 256] = dot(given, order).astype(bf16)
+
+    def finish(flat, at):
+        at = pl.ds(pl.multiple_of(at, 128), 128)
+        sig = sigmoid(flat)
+        slope[:, at] = sig * (1.0 + flat * (1.0 - sig))
+        top = (flat * sig).astype(bf16)
+        for m in range(MICRO):
+            tokens_of = dot(expand[m], top[m * slots : (m + 1) * slots])
+            flow[m * count : (m + 1) * count, at] = tokens_of.astype(bf16)
+
+    def project_x(offset, c):
+        i = lax.rem(x + offset, NX)
+        finish(dot(given, wout[i, c, 0].reshape(columns, 128)), i * 512 + c * 256)
+
+    def project_y(offset, which):
+        i, c = y_peer(offset), (core, other)[which]
+        block = jnp.concatenate([wout[n, c, 1, :, i].reshape(16 * nz, 128) for n in range(NX)], axis=1)
+        mine = given_y[:, pl.ds(pl.multiple_of(i * 256, 256), 256)]
+        if offset == 0:
+            sums[which] = dot(mine, block)
+        else:
+            sums[which] += dot(mine, block)
+
+    def project_rest(which):
+        c = (core, other)[which]
+        for n in range(NX):
+            finish(sums[which, :, 128 * n : 128 * n + 128], n * 512 + c * 256 + 128)
+
+    def project(offsets):
+        for offset in offsets:
+            project_x(offset, core)
+            project_y(offset, 0)
+        if offsets[-1] == 2:
+            project_rest(0)
+        for offset in offsets:
+            for ring in (2, 3):
+                across(ring, offset, mine=False).wait_recv()
+            project_x(offset, other)
+            project_y(offset, 1)
+        if offsets[-1] == 2:
+            project_rest(1)
+
+    project((0,))
+    for ring in (2, 3):
+        ring_second(ring)
+        start(across(ring, 3))
+        start(across(ring, 1))
+    project((3, 1))
 
     i32 = jnp.int32
     live = lax.broadcasted_iota(i32, (DCAP, 64), 0) < tally_ref[...]
@@ -340,10 +402,6 @@
     scale = jnp.concatenate([scale[:64], jnp.where(row < limit, 0.0, scale[64:])], axis=0)
 
     for ring in (2, 3):
-        ring_second(ring)
-        start(across(ring, 3))
-        start(across(ring, 1))
-    for ring in (2, 3):
         ring_third(ring)
         start(across(ring, 2))
 
@@ -352,9 +410,7 @@
     for p in range(SHARDS):
         line = slice(64 + DCAP * p, 64 + DCAP * p + DCAP)
         mom_send[p] = jnp.concatenate([first_ref[line], second_ref[line]], axis=0).astype(bf16)
-    for ring in (2, 3):
-        for offset in (0, 3, 1, 2):
-            across(ring, offset, mine=False).wait_recv()
+    project((2,))
     for k in across_table:
         p = table_peer(k)
         start(remote(mom_send.at[p], mom_got.at[shard], m_s.at[k], m_r.at[shard], (dp, p)))
@@ -366,18 +422,6 @@
     def weight(i):
         sides = [wout[i // 2, i % 2, g].reshape(columns, 128) for g in range(2)]
         return jnp.concatenate(sides, axis=1)
-
-    for i in range(8):
-        flat = dot(given, weight(i))
-        sig = sigmoid(flat)
-        value = flat * sig
-        slope[:, 256 * i : 256 * i + 256] = sig * (1.0 + flat * (1.0 - sig))
-        top = value.astype(bf16)
-        for m in range(MICRO):
-            span = slice(m * count, (m + 1) * count)
-            part = slice(m * slots, (m + 1) * slots)
-            spread = dot(expand[m], top[part])
-            flow[span, 256 * i : 256 * i + 256] = spread.astype(bf16)
 
     def slot_send(piece, src, to, k, p):
         m = min(piece, 1)
@@ -478,6 +522,7 @@
         half_sums(h)
         for k in across_y:
             start(half_y(h, y_peer(k), y, k))
+    drain()
     for h in range(2):
         part = slice(h * tiles, (h + 1) * tiles)
         y_sum = y_send[y, part].astype(f32)
@@ -556,6 +601,7 @@
             second_out[span, over] = beta_two * second_ref[span, over] + (1.0 - beta_two) * (
                 grad[n] * grad[n]
             )
+    drain()
     for h in range(2):
         over = slice(h * side, (h + 1) * side)
         for k in reversed(across_table):
@@ -628,6 +674,8 @@
             pltpu.VMEM(table.shape, f32),
             pltpu.VMEM((SHARDS, MICRO, CAP, columns), bf16),
             pltpu.VMEM((SHARDS, MICRO, CAP, columns), bf16),
+            pltpu.VMEM((MICRO * slots, columns), bf16),
+            pltpu.VMEM((2, MICRO * slots, 512), f32),
             pltpu.VMEM((MICRO * slots, 2048), f32),
             pltpu.VMEM((tokens, 2048), bf16),
             pltpu.VMEM((HEADS, count, count), bf16),

time: 98.8 us -> 96 us (0.972)
  Pallas kernels: 95.6 us -> 92.7 us
    pallas_call x1, Pallas kernels: 95.6 us -> 92.7 us  [body(): pl.pallas_call(functools.partial(whole_kernel, nz), out_shape=(jax.ShapeD...]
where the time goes in v3:
time: 96 us; the launch traced here: 95.8 us
  Pallas kernels  92.7 us (97%)
  other arithmetic  2.46 us (3%)
    pallas_call x1, Pallas kernels, body(): pl.pallas_call(functools.partial(whole_kernel, nz), out_shape=(jax.ShapeD...  92.7 us
    convert_element_type x1, other arithmetic, body(): return (jnp.where(keep, update, 0.0).astype(bf16), new_first, new_second)  2.46 us

profile of v3, /device:TPU:1, one launch (start us, length us, event | category | flops | bytes accessed | tf_op | source)
XLA Modules:
  0.0 95.8 jit_solution(7582540331831973550)
XLA Ops:
  0.6 0.0 copy-start
  0.6 92.7 %whole.1 = (f32[128,1024]{1,0:T(8,128)}, f32[128,1024]{1,0:T(8,128)}) custom-call(s32[2,8,16]{2,1,0:T(8,128)} %req_hbm.1, s32[2,1,256]{2,1,0:T(1,128)} %slot_hbm.1, s32[2,1,256]{2,1,0:T(1,128)} %seg_hbm.1, s32[1,64]{1,0:T(1,128)} %bitcast.3, s32[8,64]{1,0:T(8,128)} %bitcast.2, bf16[128,1024]{1,0:T(8,128)(2,1)} %table_hbm.1, bf16[16,2048]{1,0:T(8,128)(2,1)} %w_hbm.1, ...), custom_call_target="tpu_custom_call" | custom-call | tf_op jit(solution)/shard_map/whole/pallas_call | solution.py:654
  93.4 0.0 copy-done
  93.4 2.5 %select_convert_fusion = (bf16[128,1024]{1,0:T(8,128)(2,1)}, f32[128,1024]{1,0:T(8,128)}, f32[128,1024]{1,0:T(8,128)}) fusion(bf16[128,1024]{1,0:T(8,128)(2,1)S(1)} %copy-done, f32[128,1024]{1,0:T(8,128)} %get-tuple-element.5, f32[128,1024]{1,0:T(8,128)} %get-tuple-element.6), kind=kLoop, calls=%fused_computation | loop fusion | flops 1310720 | bytes 2621440 | tf_op jit(solution)/shard_map/convert_element_type | solution.py:742
Async XLA Ops:
  0.6 92.7 %copy-start = (bf16[128,1024]{1,0:T(8,128)(2,1)S(1)}, bf16[128,1024]{1,0:T(8,128)(2,1)}, u32[]{:S(2)}) copy-start(bf16[128,1024]{1,0:T(8,128)(2,1)} %table_hbm.1) | copy-start | bytes 786436

commit v4 on v3

--- a/solution.py
+++ b/solution.py
@@ -37,7 +37,7 @@
     barrier = pltpu.get_barrier_semaphore()
     for peer in peers:
         pl.semaphore_signal(barrier, inc=1, device_id=peer, device_id_type=MESH)
-    pl.semaphore_wait(barrier, len(peers))
+    return barrier, len(peers)
 
 
 def remote(src, dst, send, recv, peer):
@@ -173,6 +173,12 @@
         across_z += [k, nz - k]
     across_y = (2, 1, 3)
 
+    barrier = greet(
+        [(dp, table_peer(k)) for k in range(1, SHARDS)]
+        + [(z_peer(k) * NY + y, shard) for k in range(1, nz)]
+        + [along_y(k) for k in range(1, NY)]
+    )
+
     local = [(req_hbm, req_ref)]
     for g in range(2):
         part = pl.ds(pl.multiple_of(shard * 256 + g * 128, 128), 128)
@@ -191,6 +197,27 @@
     for copy in local:
         copy.start()
 
+    pl.semaphore_wait(*barrier)
+
+    started = []
+
+    def start(copy):
+        copy.start()
+        started.append(copy)
+        return copy
+
+    def drain():
+        for copy in started:
+            copy.wait_send()
+        started.clear()
+
+    local[1].wait()
+    local[2].wait()
+    for k in across_z:
+        q = z_peer(k)
+        block = wout.at[x, core, :, z, y]
+        start(remote(block, block, z_s.at[k], z_r.at[z], (q * NY + y, shard)))
+
     local[0].wait()
     lane = lax.broadcasted_iota(jnp.int32, (CAP, 128), 1) % 32
     deep = lax.broadcasted_iota(jnp.int32, (CAP, 128), 0)
@@ -202,32 +229,6 @@
     wide = jnp.where(mine, wide.astype(jnp.int32), -1)
     for p in range(SHARDS):
         asked[p] = jnp.broadcast_to(wide[p : p + 1], (8, 128))
-
-    greet(
-        [(dp, table_peer(k)) for k in range(1, SHARDS)]
-        + [(z_peer(k) * NY + y, shard) for k in range(1, nz)]
-        + [along_y(k) for k in range(1, NY)]
-    )
-
-    started = []
-
-    def start(copy):
-        copy.start()
-        started.append(copy)
-        return copy
-
-    def drain():
-        for copy in started:
-            copy.wait_send()
-        started.clear()
-
-    local[1].wait()
-    local[2].wait()
-    for k in across_z:
-        q = z_peer(k)
-        block = wout.at[x, core, :, z, y]
-        start(remote(block, block, z_s.at[k], z_r.at[z], (q * NY + y, shard)))
-
     for k in across_table:
         p = table_peer(k)
         start(remote(asked.at[p], held.at[shard], req_s.at[k], req_r.at[shard], (dp, p)))
@@ -287,12 +288,18 @@
         s = (ring - 2) * 4 + offset
         return remote(block, block, core_s.at[s], core_r.at[s], (dp, x * 2 + other))
 
-    for ring in (0, 1):
-        ring_first(ring)
-    for ring in (0, 1):
-        ring_second(ring)
-    for ring in (0, 1):
-        ring_third(ring)
+    def middle(ring, which, offset):
+        block = views[ring](lax.rem(spots[ring] + offset, 4), whole)
+        return remote(
+            block, block, ring_s.at[ring, which], ring_r.at[ring, which], steps[ring](which)
+        )
+
+    for which in (2, 1, 3):
+        for ring in (0, 1):
+            start(middle(ring, which, 0))
+    for which in (1, 3, 2):
+        for ring in (0, 1):
+            middle(ring, which, 4 - which).wait_recv()
     for ring in (2, 3):
         ring_first(ring)
         start(across(ring, 0))

time: 96 us -> 95.5 us (level)
  no operation moved by 1% of the time
where the time goes in v4:
time: 95.5 us; the launch traced here: 95.3 us
  Pallas kernels  92.2 us (97%)
  other arithmetic  2.46 us (3%)
    pallas_call x1, Pallas kernels, body(): pl.pallas_call(functools.partial(whole_kernel, nz), out_shape=(jax.ShapeD...  92.2 us
    convert_element_type x1, other arithmetic, body(): return (jnp.where(keep, update, 0.0).astype(bf16), new_first, new_second)  2.46 us

profile of v4, /device:TPU:1, one launch (start us, length us, event | category | flops | bytes accessed | tf_op | source)
XLA Modules:
  0.0 95.3 jit_solution(4996684745231246165)
XLA Ops:
  0.6 0.0 copy-start
  0.6 92.2 %whole.1 = (f32[128,1024]{1,0:T(8,128)}, f32[128,1024]{1,0:T(8,128)}) custom-call(s32[2,8,16]{2,1,0:T(8,128)} %req_hbm.1, s32[2,1,256]{2,1,0:T(1,128)} %slot_hbm.1, s32[2,1,256]{2,1,0:T(1,128)} %seg_hbm.1, s32[1,64]{1,0:T(1,128)} %bitcast.3, s32[8,64]{1,0:T(8,128)} %bitcast.2, bf16[128,1024]{1,0:T(8,128)(2,1)} %table_hbm.1, bf16[16,2048]{1,0:T(8,128)(2,1)} %w_hbm.1, ...), custom_call_target="tpu_custom_call" | custom-call | tf_op jit(solution)/shard_map/whole/pallas_call | solution.py:661
  92.9 0.0 copy-done
  92.9 2.5 %select_convert_fusion = (bf16[128,1024]{1,0:T(8,128)(2,1)}, f32[128,1024]{1,0:T(8,128)}, f32[128,1024]{1,0:T(8,128)}) fusion(bf16[128,1024]{1,0:T(8,128)(2,1)S(1)} %copy-done, f32[128,1024]{1,0:T(8,128)} %get-tuple-element.5, f32[128,1024]{1,0:T(8,128)} %get-tuple-element.6), kind=kLoop, calls=%fused_computation | loop fusion | flops 1310720 | bytes 2621440 | tf_op jit(solution)/shard_map/convert_element_type | solution.py:749
Async XLA Ops:
  0.6 92.2 %copy-start = (bf16[128,1024]{1,0:T(8,128)(2,1)S(1)}, bf16[128,1024]{1,0:T(8,128)(2,1)}, u32[]{:S(2)}) copy-start(bf16[128,1024]{1,0:T(8,128)(2,1)} %table_hbm.1) | copy-start | bytes 786436

commit v5 on v4

--- a/solution.py
+++ b/solution.py
@@ -246,67 +246,6 @@
         start(remote(found.at[p], fetched.at[shard], fnd_s.at[k], fnd_r.at[shard], (dp, p)))
     fetched[shard] = found[shard]
 
-    for k in reversed(across_z):
-        q = z_peer(k)
-        block = wout.at[x, core, :, q, y]
-        remote(block, block, z_s.at[k], z_r.at[q], (q * NY + y, shard)).wait_recv()
-
-    whole, low, high = pl.ds(0, nz), pl.ds(0, half), pl.ds(half, half)
-    views = (
-        lambda i, zs: wout.at[x, core, 0, zs, i],
-        lambda i, zs: wout.at[i, core, 1, zs, y],
-        lambda i, zs: wout.at[i, core, 0, zs],
-        lambda i, zs: wout.at[:, core, 1, zs, i],
-    )
-    spots = (y, x, x, y)
-    steps = (along_y, along_x, along_x, along_y)
-
-    def link(ring, which, offset, zs, to):
-        block = views[ring](lax.rem(spots[ring] + offset, 4), zs)
-        return remote(
-            block, block, ring_s.at[ring, which], ring_r.at[ring, which], steps[ring](to)
-        )
-
-    def ring_first(ring):
-        start(link(ring, 0, 0, whole, 1))
-        start(link(ring, 1, 0, whole, 3))
-
-    def ring_second(ring):
-        link(ring, 0, 3, whole, 1).wait_recv()
-        start(link(ring, 2, 3, low, 1))
-        link(ring, 1, 1, whole, 3).wait_recv()
-        start(link(ring, 3, 1, high, 3))
-
-    def ring_third(ring):
-        link(ring, 2, 2, low, 1).wait_recv()
-        link(ring, 3, 2, high, 3).wait_recv()
-
-    def across(ring, offset, mine=True):
-        i = lax.rem(spots[ring] + offset, 4)
-        c = core if mine else other
-        block = wout.at[i, c, 0] if ring == 2 else wout.at[:, c, 1, :, i]
-        s = (ring - 2) * 4 + offset
-        return remote(block, block, core_s.at[s], core_r.at[s], (dp, x * 2 + other))
-
-    def middle(ring, which, offset):
-        block = views[ring](lax.rem(spots[ring] + offset, 4), whole)
-        return remote(
-            block, block, ring_s.at[ring, which], ring_r.at[ring, which], steps[ring](which)
-        )
-
-    for which in (2, 1, 3):
-        for ring in (0, 1):
-            start(middle(ring, which, 0))
-    for which in (1, 3, 2):
-        for ring in (0, 1):
-            middle(ring, which, 4 - which).wait_recv()
-    for ring in (2, 3):
-        ring_first(ring)
-        start(across(ring, 0))
-
-    for k in reversed(across_table):
-        p = table_peer(k)
-        remote(found.at[p], fetched.at[p], fnd_s.at[k], fnd_r.at[p], (dp, p)).wait_recv()
     for copy in local[7:]:
         copy.wait()
     count = seg_ref.shape[2]
@@ -325,66 +264,6 @@
         same = dot(belongs, belongs, ((0,), (0,)))
         history = jnp.sum(same, axis=1, keepdims=True)
         share.append(jnp.where(causal, same, 0.0) / history)
-    rows = jnp.concatenate(
-        [fetched[:, m].reshape(slots, columns) for m in range(MICRO)], axis=0
-    ).astype(f32)
-    normed, factor = normalise(rows)
-    given = normed.astype(bf16)
-    lane = lax.broadcasted_iota(jnp.int32, (1, columns), 1)
-    deep = lax.broadcasted_iota(jnp.int32, (columns, 256), 0)
-    for i in range(NY):
-        j = lane[:, 256 * i : 256 * i + 256]
-        origin = ((j // 16) % nz) * (NY * 16) + (j // (16 * nz)) * 16 + j % 16
-        order = jnp.where(deep == origin, 1.0, 0.0).astype(bf16)
-        given_y[:, 256 * i : 256 * i + 256] = dot(given, order).astype(bf16)
-
-    def finish(flat, at):
-        at = pl.ds(pl.multiple_of(at, 128), 128)
-        sig = sigmoid(flat)
-        slope[:, at] = sig * (1.0 + flat * (1.0 - sig))
-        top = (flat * sig).astype(bf16)
-        for m in range(MICRO):
-            tokens_of = dot(expand[m], top[m * slots : (m + 1) * slots])
-            flow[m * count : (m + 1) * count, at] = tokens_of.astype(bf16)
-
-    def project_x(offset, c):
-        i = lax.rem(x + offset, NX)
-        finish(dot(given, wout[i, c, 0].reshape(columns, 128)), i * 512 + c * 256)
-
-    def project_y(offset, which):
-        i, c = y_peer(offset), (core, other)[which]
-        block = jnp.concatenate([wout[n, c, 1, :, i].reshape(16 * nz, 128) for n in range(NX)], axis=1)
-        mine = given_y[:, pl.ds(pl.multiple_of(i * 256, 256), 256)]
-        if offset == 0:
-            sums[which] = dot(mine, block)
-        else:
-            sums[which] += dot(mine, block)
-
-    def project_rest(which):
-        c = (core, other)[which]
-        for n in range(NX):
-            finish(sums[which, :, 128 * n : 128 * n + 128], n * 512 + c * 256 + 128)
-
-    def project(offsets):
-        for offset in offsets:
-            project_x(offset, core)
-            project_y(offset, 0)
-        if offsets[-1] == 2:
-            project_rest(0)
-        for offset in offsets:
-            for ring in (2, 3):
-                across(ring, offset, mine=False).wait_recv()
-            project_x(offset, other)
-            project_y(offset, 1)
-        if offsets[-1] == 2:
-            project_rest(1)
-
-    project((0,))
-    for ring in (2, 3):
-        ring_second(ring)
-        start(across(ring, 3))
-        start(across(ring, 1))
-    project((3, 1))
 
     i32 = jnp.int32
     live = lax.broadcasted_iota(i32, (DCAP, 64), 0) < tally_ref[...]
@@ -408,15 +287,138 @@
     scale = 1.0 / (1.0 + tally)
     scale = jnp.concatenate([scale[:64], jnp.where(row < limit, 0.0, scale[64:])], axis=0)
 
-    for ring in (2, 3):
-        ring_third(ring)
-        start(across(ring, 2))
-
     for copy in local[4:7]:
         copy.wait()
     for p in range(SHARDS):
         line = slice(64 + DCAP * p, 64 + DCAP * p + DCAP)
         mom_send[p] = jnp.concatenate([first_ref[line], second_ref[line]], axis=0).astype(bf16)
+
+    for k in reversed(across_z):
+        q = z_peer(k)
+        block = wout.at[x, core, :, q, y]
+        remote(block, block, z_s.at[k], z_r.at[q], (q * NY + y, shard)).wait_recv()
+
+    whole, low, high = pl.ds(0, nz), pl.ds(0, half), pl.ds(half, half)
+    views = (
+        lambda i, zs: wout.at[x, core, 0, zs, i],
+        lambda i, zs: wout.at[i, core, 1, zs, y],
+        lambda i, zs: wout.at[i, core, 0, zs],
+        lambda i, zs: wout.at[:, core, 1, zs, i],
+    )
+    spots = (y, x, x, y)
+    steps = (along_y, along_x, along_x, along_y)
+
+    def link(ring, which, offset, zs, to):
+        block = views[ring](lax.rem(spots[ring] + offset, 4), zs)
+        return remote(
+            block, block, ring_s.at[ring, which], ring_r.at[ring, which], steps[ring](to)
+        )
+
+    def ring_first(ring):
+        start(link(ring, 0, 0, whole, 1))
+        start(link(ring, 1, 0, whole, 3))
+
+    def ring_second(ring):
+        link(ring, 0, 3, whole, 1).wait_recv()
+        start(link(ring, 2, 3, low, 1))
+        link(ring, 1, 1, whole, 3).wait_recv()
+        start(link(ring, 3, 1, high, 3))
+
+    def ring_third(ring):
+        link(ring, 2, 2, low, 1).wait_recv()
+        link(ring, 3, 2, high, 3).wait_recv()
+
+    def across(ring, offset, mine=True):
+        i = lax.rem(spots[ring] + offset, 4)
+        c = core if mine else other
+        block = wout.at[i, c, 0] if ring == 2 else wout.at[:, c, 1, :, i]
+        s = (ring - 2) * 4 + offset
+        return remote(block, block, core_s.at[s], core_r.at[s], (dp, x * 2 + other))
+
+    def middle(ring, which, offset):
+        block = views[ring](lax.rem(spots[ring] + offset, 4), whole)
+        return remote(
+            block, block, ring_s.at[ring, which], ring_r.at[ring, which], steps[ring](which)
+        )
+
+    for which in (2, 1, 3):
+        for ring in (0, 1):
+            start(middle(ring, which, 0))
+    for which in (1, 3, 2):
+        for ring in (0, 1):
+            middle(ring, which, 4 - which).wait_recv()
+    for ring in (2, 3):
+        ring_first(ring)
+        start(across(ring, 0))
+
+    for k in reversed(across_table):
+        p = table_peer(k)
+        remote(found.at[p], fetched.at[p], fnd_s.at[k], fnd_r.at[p], (dp, p)).wait_recv()
+    rows = jnp.concatenate(
+        [fetched[:, m].reshape(slots, columns) for m in range(MICRO)], axis=0
+    ).astype(f32)
+    normed, factor = normalise(rows)
+    given = normed.astype(bf16)
+    lane = lax.broadcasted_iota(jnp.int32, (1, columns), 1)
+    deep = lax.broadcasted_iota(jnp.int32, (columns, 256), 0)
+    for i in range(NY):
+        j = lane[:, 256 * i : 256 * i + 256]
+        origin = ((j // 16) % nz) * (NY * 16) + (j // (16 * nz)) * 16 + j % 16
+        order = jnp.where(deep == origin, 1.0, 0.0).astype(bf16)
+        given_y[:, 256 * i : 256 * i + 256] = dot(given, order).astype(bf16)
+
+    def finish(flat, at):
+        at = pl.ds(pl.multiple_of(at, 128), 128)
+        sig = sigmoid(flat)
+        slope[:, at] = sig * (1.0 + flat * (1.0 - sig))
+        top = (flat * sig).astype(bf16)
+        for m in range(MICRO):
+            tokens_of = dot(expand[m], top[m * slots : (m + 1) * slots])
+            flow[m * count : (m + 1) * count, at] = tokens_of.astype(bf16)
+
+    def project_x(offset, c):
+        i = lax.rem(x + offset, NX)
+        finish(dot(given, wout[i, c, 0].reshape(columns, 128)), i * 512 + c * 256)
+
+    def project_y(offset, which):
+        i, c = y_peer(offset), (core, other)[which]
+        block = jnp.concatenate([wout[n, c, 1, :, i].reshape(16 * nz, 128) for n in range(NX)], axis=1)
+        mine = given_y[:, pl.ds(pl.multiple_of(i * 256, 256), 256)]
+        if offset == 0:
+            sums[which] = dot(mine, block)
+        else:
+            sums[which] += dot(mine, block)
+
+    def project_rest(which):
+        c = (core, other)[which]
+        for n in range(NX):
+            finish(sums[which, :, 128 * n : 128 * n + 128], n * 512 + c * 256 + 128)
+
+    def project(offsets):
+        for offset in offsets:
+            project_x(offset, core)
+            project_y(offset, 0)
+        if offsets[-1] == 2:
+            project_rest(0)
+        for offset in offsets:
+            for ring in (2, 3):
+                across(ring, offset, mine=False).wait_recv()
+            project_x(offset, other)
+            project_y(offset, 1)
+        if offsets[-1] == 2:
+            project_rest(1)
+
+    project((0,))
+    for ring in (2, 3):
+        ring_second(ring)
+        start(across(ring, 3))
+        start(across(ring, 1))
+    project((3, 1))
+
+    for ring in (2, 3):
+        ring_third(ring)
+        start(across(ring, 2))
+
     project((2,))
     for k in across_table:
         p = table_peer(k)

time: 95.5 us -> 95.6 us (level)
  no operation moved by 1% of the time
where the time goes in v5:
time: 95.6 us; the launch traced here: 95.4 us
  Pallas kernels  92.3 us (97%)
  other arithmetic  2.46 us (3%)
    pallas_call x1, Pallas kernels, body(): pl.pallas_call(functools.partial(whole_kernel, nz), out_shape=(jax.ShapeD...  92.3 us
    convert_element_type x1, other arithmetic, body(): return (jnp.where(keep, update, 0.0).astype(bf16), new_first, new_second)  2.46 us

profile of v5, /device:TPU:1, one launch (start us, length us, event | category | flops | bytes accessed | tf_op | source)
XLA Modules:
  0.0 95.4 jit_solution(12475161321423979976)
XLA Ops:
  0.6 0.0 copy-start
  0.6 92.3 %whole.1 = (f32[128,1024]{1,0:T(8,128)}, f32[128,1024]{1,0:T(8,128)}) custom-call(s32[2,8,16]{2,1,0:T(8,128)} %req_hbm.1, s32[2,1,256]{2,1,0:T(1,128)} %slot_hbm.1, s32[2,1,256]{2,1,0:T(1,128)} %seg_hbm.1, s32[1,64]{1,0:T(1,128)} %bitcast.3, s32[8,64]{1,0:T(8,128)} %bitcast.2, bf16[128,1024]{1,0:T(8,128)(2,1)} %table_hbm.1, bf16[16,2048]{1,0:T(8,128)(2,1)} %w_hbm.1, ...), custom_call_target="tpu_custom_call" | custom-call | tf_op jit(solution)/shard_map/whole/pallas_call | solution.py:663
  93.0 0.0 copy-done
  93.0 2.5 %select_convert_fusion = (bf16[128,1024]{1,0:T(8,128)(2,1)}, f32[128,1024]{1,0:T(8,128)}, f32[128,1024]{1,0:T(8,128)}) fusion(bf16[128,1024]{1,0:T(8,128)(2,1)S(1)} %copy-done, f32[128,1024]{1,0:T(8,128)} %get-tuple-element.5, f32[128,1024]{1,0:T(8,128)} %get-tuple-element.6), kind=kLoop, calls=%fused_computation | loop fusion | flops 1310720 | bytes 2621440 | tf_op jit(solution)/shard_map/convert_element_type | solution.py:751
Async XLA Ops:
  0.6 92.3 %copy-start = (bf16[128,1024]{1,0:T(8,128)(2,1)S(1)}, bf16[128,1024]{1,0:T(8,128)(2,1)}, u32[]{:S(2)}) copy-start(bf16[128,1024]{1,0:T(8,128)(2,1)} %table_hbm.1) | copy-start | bytes 786436
